TPU v7x, 32 devices: a whole 2x2x4 slice. The times are simulated.
32 devices in a mesh: side: 2 (over core), grp: 4 (over y, x), head: 4 (over z).
Axes of the slice: x: 2, y: 2, z: 4, core: 2. Of those that a mesh axis runs over, the one named last changes fastest.
Arguments:
- q_new: bfloat16 [8, 64, 4096], P(('side', 'grp'), None, 'head'), may hold values from -12 to 12
- k_cache: bfloat16 [8, 4, 512, 128], P(('side', 'grp'), 'head'), may hold values from -12 to 12
- value_cache: bfloat16 [8, 4, 512, 128], P(('side', 'grp'), 'head'), may hold values from -12 to 12
- k_new: bfloat16 [8, 64, 512], P(('side', 'grp'), None, 'head'), may hold values from -12 to 12
- new_value_rows: bfloat16 [8, 64, 512], P(('side', 'grp'), None, 'head'), may hold values from -12 to 12
- cache_len: int32 [8], P(('side', 'grp')), may hold values from 1 to 512, 2048 in all
- hidden_in: bfloat16 [8, 64, 2048], P(('side', 'grp'), 'head'), may hold values from -8 to 8
- out_proj: bfloat16 [4096, 2048], P('head', 'side'), may hold values from -0.09375 to 0.09375
- norm_gain: float32 [2048], replicated, may hold values from 0.1 to 1.9
- expert_ids: int32 [8, 64, 8], P(('side', 'grp'), 'head'), may hold values from 0 to 7, all different within a row; in each aligned block of 16 rows (0 to 15, 16 to 31, ..., all dimensions but the last counted through in order) at most 16 rows name the same one
- gate_wts: float32 [8, 64, 8], P(('side', 'grp'), 'head'), may hold values from 0.05 to 1
- w_gate: bfloat16 [8, 2048, 768], P(('side', 'grp'), None, 'head'), may hold values from -0.125 to 0.125
- w_up: bfloat16 [8, 2048, 768], P(('side', 'grp'), None, 'head'), may hold values from -0.125 to 0.125
- w_down: bfloat16 [8, 768, 2048], P(('side', 'grp'), 'head'), may hold values from -0.21875 to 0.21875
Outputs:
- layer_out: bfloat16 [8, 64, 2048], P(('side', 'grp'), 'head')
Inputs may be any that keep to these rules, and one draw needn't show every extreme that they name: `expert_ids`: each row names 8 different experts. In each aligned block of 16 rows (one stream's rows taken 16 at a time) no expert is named by more than 16 rows, a bound that some block reaches. `cache_len`: some stream has all 512 positions valid.
All inputs are finite; a program needn't handle non-finite values. No bound on the sum of `cache_len` on one device may be relied on, other than what follows from the above.
Results may differ from a plain program's by a relative error of at most 0.015.
Values may be sent and summed in bfloat16 or wider, within the bound.
A program may use at most 64 MiB of HBM per device.

v0:
```python
import math

import jax
import jax.numpy as jnp
from jax import lax
from jax.sharding import PartitionSpec as P


def attend(q_new, k_cache, value_cache, k_new, new_value_rows, cache_len):
    q_rows = q_new.shape[1]
    head_dim = k_cache.shape[3]
    cached_part = k_cache.shape[2]
    query_groups = q_new.shape[2] // head_dim
    joined_keys = jnp.concatenate([k_cache[0, 0], k_new[0]], axis=0)
    joined_values = jnp.concatenate([value_cache[0, 0], new_value_rows[0]], axis=0)
    query_rows = q_new[0].reshape(q_rows, query_groups, head_dim)
    scores = jnp.einsum(
        "rgd,kd->grk", query_rows, joined_keys, preferred_element_type=jnp.float32
    ) / math.sqrt(head_dim)
    key_pos = jnp.arange(cached_part + q_rows)[None, :]
    row_pos = jnp.arange(q_rows)[:, None]
    visible = jnp.where(
        key_pos < cached_part, key_pos < cache_len[0], key_pos - cached_part <= row_pos
    )
    scores = jnp.where(visible[None], scores, -jnp.inf)
    highest = jnp.max(scores, axis=-1, keepdims=True)
    exp_scores = jnp.exp(scores - highest)
    attn_probs = (exp_scores / jnp.sum(exp_scores, axis=-1, keepdims=True)).astype(jnp.bfloat16)
    context = jnp.einsum(
        "grk,kd->rgd", attn_probs, joined_values, preferred_element_type=jnp.float32
    ).astype(jnp.bfloat16)
    return context.reshape(q_rows, query_groups * head_dim)


def routing_tables(chosen, mixing, experts, most):
    rows_here, top_k = chosen.shape
    one_hot = (
        (chosen[:, :, None] == jnp.arange(experts)[None, None, :])
        .astype(jnp.int32)
        .reshape(rows_here * top_k, experts)
    )
    earlier = jnp.cumsum(one_hot, axis=0) - one_hot
    slot_index = jnp.sum(earlier * one_hot, axis=1)
    target = chosen.reshape(-1) * most + slot_index
    matches = (jnp.arange(experts * most)[:, None] == target[None, :]).reshape(
        experts * most, rows_here, top_k
    )
    dispatch = jnp.any(matches, axis=2).astype(jnp.bfloat16)
    combine = jnp.sum(jnp.where(matches, mixing.astype(jnp.float32)[None], 0.0), axis=2).T.astype(
        jnp.bfloat16
    )
    return (dispatch, combine)


def shards(
    q_new,
    k_cache,
    value_cache,
    k_new,
    new_value_rows,
    cache_len,
    hidden_in,
    out_proj,
    norm_gain,
    expert_ids,
    gate_wts,
    w_gate,
    w_up,
    w_down,
):
    context = attend(q_new, k_cache, value_cache, k_new, new_value_rows, cache_len)
    width = hidden_in.shape[2]
    halves = jnp.einsum(
        "sre,ec->src",
        lax.all_gather(context[None], "side", axis=0, tiled=True),
        out_proj,
        preferred_element_type=jnp.float32,
    )
    summed = lax.psum_scatter(
        halves.astype(jnp.bfloat16), "head", scatter_dimension=1, tiled=True
    ).astype(jnp.float32)
    attn_out = lax.all_to_all(
        summed.astype(jnp.bfloat16), "side", split_axis=0, concat_axis=2, tiled=True
    ).astype(summed.dtype)[0]
    resid = hidden_in[0].astype(jnp.float32) + attn_out
    normed = (
        resid * lax.rsqrt(jnp.mean(resid * resid, axis=-1, keepdims=True) + 1e-06) * norm_gain
    ).astype(jnp.bfloat16)
    raw_wts = gate_wts[0]
    mixing = (raw_wts / jnp.sum(raw_wts, axis=-1, keepdims=True)).astype(jnp.bfloat16)
    experts = lax.axis_size("side") * lax.axis_size("grp")
    quarters = lax.axis_size("head")
    rows_here = expert_ids.shape[1]
    top_k = expert_ids.shape[2]
    most = max(2, (rows_here * top_k + experts - 1) // experts)
    dispatch, combine = routing_tables(expert_ids[0], mixing, experts, most)
    group_rows, group_dispatch = (
        lax.all_gather(normed[None], "head", axis=0, tiled=True),
        lax.all_gather(dispatch[None], "head", axis=0, tiled=True),
    )
    outgoing = (
        jnp.einsum("hsr,hrd->hsd", group_dispatch, group_rows, preferred_element_type=jnp.float32)
        .astype(jnp.bfloat16)
        .reshape(quarters, experts, most, width)
    )
    slot_rows = lax.all_to_all(outgoing, ("side", "grp"), split_axis=1, concat_axis=1, tiled=True)
    flat_rows = slot_rows.reshape(-1, width)
    gate_proj = jnp.dot(flat_rows, w_gate[0], preferred_element_type=jnp.float32)
    up_proj = jnp.dot(flat_rows, w_up[0], preferred_element_type=jnp.float32)
    hidden = (jax.nn.silu(gate_proj) * up_proj).astype(jnp.bfloat16)
    partial_value = (
        jnp.dot(hidden, w_down[0], preferred_element_type=jnp.float32)
        .astype(jnp.bfloat16)
        .reshape(quarters, experts, most, width)
    )
    combine_all = lax.all_gather(combine[None], "head", axis=0, tiled=True)
    returned = lax.all_to_all(
        partial_value, ("side", "grp"), split_axis=1, concat_axis=1, tiled=True
    )
    weighted = jnp.einsum(
        "hrs,hsd->hrd",
        combine_all,
        returned.reshape(quarters, experts * most, width),
        preferred_element_type=jnp.float32,
    )
    moe_out = lax.psum_scatter(
        weighted.astype(jnp.bfloat16), "head", scatter_dimension=0, tiled=True
    ).astype(jnp.float32)[0]
    return (resid + moe_out).astype(jnp.bfloat16)[None]


def solution(mesh):
    in_specs = (
        P(("side", "grp"), None, "head"),
        P(("side", "grp"), "head", None, None),
        P(("side", "grp"), "head", None, None),
        P(("side", "grp"), None, "head"),
        P(("side", "grp"), None, "head"),
        P(("side", "grp")),
        P(("side", "grp"), "head", None),
        P("head", "side"),
        P(),
        P(("side", "grp"), "head", None),
        P(("side", "grp"), "head", None),
        P(("side", "grp"), None, "head"),
        P(("side", "grp"), None, "head"),
        P(("side", "grp"), "head", None),
    )
    out_specs = P(("side", "grp"), "head", None)
    return jax.shard_map(shards, mesh=mesh, in_specs=in_specs, out_specs=out_specs, check_vma=False)
```

profile of v0, /device:TPU:0, one launch (start us, length us, event | category | flops | bytes accessed | tf_op | source)
XLA Modules:
  0.0 156.4 jit_solution(14125958922534045559)
XLA Ops:
  6.5 0.0 copy-start
  6.5 0.0 reduce-scatter.3.cloned.1.call-start
  7.4 0.9 copy.69
  8.4 1.6 fusion.58
  10.0 1.2 fusion.11
  11.2 0.0 copy-start.3
  11.2 0.1 copy.55
  11.3 0.1 broadcast_in_dim_reshape.3
  11.4 2.1 %all_gather.12 = bf16[2,64,1024]{2,1,0:T(8,128)(2,1)S(1)} all-gather(bf16[1,64,1024]{2,1,0:T(8,128)(2,1)S(1)} %broadcast_in_dim_reshape.3), channel_id=1, replica_groups=mesh['side'=2,'grp'=4,'head'=4] {'side'}, dimensions={0}, use_global_device_ids=true | all-gather | bytes 393216 | tf_op jit(solution)/shard_map/all_gather | solution.py:75
  13.5 1.1 fusion.7
  14.6 0.0 reduce-scatter.3.cloned.1.call-update
  14.7 0.1 copy.57
  14.7 0.1 eq.31
  14.8 0.1 fusion.37
  14.9 0.2 reduce_window_sum.11
  15.1 0.2 select_reduce_fusion.1
  15.3 0.1 reduce_sum.49
  15.4 0.1 copy.58
  15.4 0.1 copy.59
  15.5 0.1 fusion.38
  15.7 13.5 %all-gather.1 = bf16[512,16]{0,1:T(8,128)(2,1)S(1)} all-gather(bf16[128,16]{0,1:T(8,128)(2,1)S(1)} %convert_element_type.133), channel_id=3, replica_groups=mesh['side'=2,'grp'=4,'head'=4] {'head'}, dimensions={0}, use_global_device_ids=true | all-gather | bytes 20480 | tf_op jit(solution)/shard_map/all_gather | solution.py:99
  29.1 7.8 %reduce-scatter.3.cloned.1.call-done = bf16[2,16,1024]{2,1,0:T(8,128)(2,1)} async-done(((bf16[2,64,1024]{2,1,0:T(8,128)(2,1)}), bf16[2,16,1024]{2,1,0:T(8,128)(2,1)}) %reduce-scatter.3.cloned.1.call-update) | async-done | bytes 65552 | tf_op jit(solution)/shard_map/reduce_scatter | solution.py:79
  37.0 4.7 %all_to_all.19 = bf16[2,16,1024]{2,1,0:T(8,128)(2,1)S(1)} all-to-all(bf16[2,16,1024]{2,1,0:T(8,128)(2,1)} %reduce-scatter.3.cloned.1.call-done), channel_id=1, replica_groups=mesh['side'=2,'grp'=4,'head'=4] {'side'}, dimensions={0} | all-to-all | bytes 131072 | tf_op jit(solution)/shard_map/all_to_all | solution.py:82
  41.7 0.1 copy.56
  41.9 0.1 fusion.30
  42.0 0.0 copy-done.5
  42.0 0.1 multiply_convert_fusion
  42.1 14.5 %all_gather.15 = bf16[4,16,2048]{2,1,0:T(8,128)(2,1)S(1)} all-gather(bf16[1,16,2048]{2,1,0:T(8,128)(2,1)S(1)} %multiply_convert_fusion), channel_id=1, replica_groups=mesh['side'=2,'grp'=4,'head'=4] {'head'}, dimensions={0}, use_global_device_ids=true | all-gather | bytes 327680 | tf_op jit(solution)/shard_map/all_gather | solution.py:98
  56.6 0.7 convolution_convert_fusion.1
  57.3 0.2 copy.63
  57.5 29.8 %all_to_all.20 = bf16[4,8,16,2048]{3,2,0,1:T(8,128)(2,1)S(1)} all-to-all(bf16[4,8,16,2048]{3,2,0,1:T(8,128)(2,1)S(1)} %copy.63), channel_id=1, replica_groups=mesh['side'=2,'grp'=4,'head'=4] {'side','grp'}, dimensions={1} | all-to-all | bytes 4194304 | tf_op jit(solution)/shard_map/all_to_all | solution.py:106
  87.4 0.2 copy.64
  87.6 1.3 copy-done.1
  88.9 0.8 fusion.15
  89.8 0.3 copy-done.7
  90.1 4.7 %convolution_convert_fusion = bf16[512,2048]{1,0:T(8,128)(2,1)} fusion(bf16[512,2048]{1,0:T(8,128)(2,1)} %bitcast.105, bf16[1,192,2048]{2,1,0:T(8,128)(2,1)S(1)} %copy-done.7, bf16[1,2048,192]{1,2,0:T(8,128)(2,1)} %param.26, f32[512,192]{0,1:T(8,128)S(1)} %fusion.15), kind=kOutput, calls=%fused_computation.1 | convolution fusion | flops 806944768 | bytes 6160384 | tf_op jit(solution)/shard_map/dot_general | solution.py:112
  94.8 3.1 %copy.65 = bf16[4,8,16,2048]{3,2,0,1:T(8,128)(2,1)} copy(bf16[4,8,16,2048]{3,2,1,0:T(8,128)(2,1)} %bitcast.106) | data formatting | bytes 4194304 | tf_op jit(solution)/shard_map/reshape | solution.py:114
  97.9 4.5 %all-to-all-start.2 = ((bf16[4,8,16,2048]{3,2,0,1:T(8,128)(2,1)}), bf16[4,8,16,2048]{3,2,0,1:T(8,128)(2,1)}, u32[]{:S(2)}, u32[]{:S(2)}) async-start(bf16[4,8,16,2048]{3,2,0,1:T(8,128)(2,1)} %copy.65), calls=%async_computation.3 | async-start | bytes 4194304 | tf_op jit(solution)/shard_map/all_to_all | solution.py:117
  102.4 0.0 reduce-scatter.5.cloned.1.call-start
  102.5 0.1 copy.60
  102.5 0.1 select_reduce_fusion
  102.7 13.1 %all-gather = bf16[64,128]{1,0:T(8,128)(2,1)S(1)} all-gather(bf16[16,128]{1,0:T(8,128)(2,1)S(1)} %bitcast.115), channel_id=2, replica_groups=mesh['side'=2,'grp'=4,'head'=4] {'head'}, dimensions={0}, use_global_device_ids=true | all-gather | bytes 20480 | tf_op jit(solution)/shard_map/all_gather | solution.py:116
  115.8 12.7 %all-to-all-done.2 = bf16[4,8,16,2048]{3,2,0,1:T(8,128)(2,1)} async-done(((bf16[4,8,16,2048]{3,2,0,1:T(8,128)(2,1)}), bf16[4,8,16,2048]{3,2,0,1:T(8,128)(2,1)}, u32[]{:S(2)}, u32[]{:S(2)}) %all-to-all-start.2) | async-done | bytes 2097184 | tf_op jit(solution)/shard_map/all_to_all | solution.py:117
  128.5 1.7 %copy.66 = bf16[4,8,16,2048]{3,2,1,0:T(8,128)(2,1)S(1)} copy(bf16[4,8,16,2048]{3,2,0,1:T(8,128)(2,1)} %all-to-all-done.2) | data formatting | bytes 4194304 | tf_op jit(solution)/shard_map/all_to_all | solution.py:117
  130.2 1.1 convolution_convert_fusion.2
  131.3 0.0 reduce-scatter.5.cloned.1.call-update
  131.3 16.7 %reduce-scatter.5.cloned.1.call-done = bf16[1,16,2048]{2,1,0:T(8,128)(2,1)} async-done(((bf16[4,16,2048]{2,1,0:T(8,128)(2,1)}), bf16[1,16,2048]{2,1,0:T(8,128)(2,1)}) %reduce-scatter.5.cloned.1.call-update) | async-done | bytes 65552 | tf_op jit(solution)/shard_map/reduce_scatter | solution.py:126
  148.1 1.5 add_convert_fusion
  (30 shorter events, 0.2 us)
Async XLA Ops:
  6.5 7.0 %copy-start = (bf16[1024,1024]{1,0:T(8,128)(2,1)S(1)}, bf16[1024,1024]{1,0:T(8,128)(2,1)}, u32[]{:S(2)}) copy-start(bf16[1024,1024]{1,0:T(8,128)(2,1)} %param.21) | copy-start | bytes 6291460
  6.5 3.4 %copy-start.8 = (bf16[1,1,512,128]{3,2,1,0:T(8,128)(2,1)S(1)}, bf16[1,1,512,128]{3,2,1,0:T(8,128)(2,1)}, u32[]{:S(2)}) copy-start(bf16[1,1,512,128]{3,2,1,0:T(8,128)(2,1)} %param.15) | copy-start | bytes 393220
  6.5 3.4 %copy-start.10 = (bf16[1,64,128]{2,1,0:T(8,128)(2,1)S(1)}, bf16[1,64,128]{2,1,0:T(8,128)(2,1)}, u32[]{:S(2)}) copy-start(bf16[1,64,128]{2,1,0:T(8,128)(2,1)} %param.17) | copy-start | bytes 49156
  6.5 3.4 %copy-start.9 = (bf16[1,1,512,128]{3,2,1,0:T(8,128)(2,1)S(1)}, bf16[1,1,512,128]{3,2,1,0:T(8,128)(2,1)}, u32[]{:S(2)}) copy-start(bf16[1,1,512,128]{3,2,1,0:T(8,128)(2,1)} %param.16) | copy-start | bytes 393220
  6.5 3.4 %copy-start.11 = (bf16[1,64,128]{2,1,0:T(8,128)(2,1)S(1)}, bf16[1,64,128]{2,1,0:T(8,128)(2,1)}, u32[]{:S(2)}) copy-start(bf16[1,64,128]{2,1,0:T(8,128)(2,1)} %param.18) | copy-start | bytes 49156
  6.5 30.4 %reduce-scatter.3.cloned.1.call-start = ((), (), s32[]{:S(2)}) async-start(), calls=%async_computation.5 | async-start | bytes 327680 | tf_op jit(solution)/shard_map/reduce_scatter | solution.py:79
  11.2 3.4 %copy-start.3 = (s32[1,16,8]{1,2,0:T(8,128)S(1)}, s32[1,16,8]{1,2,0:T(8,128)}, u32[]{:S(2)}) copy-start(s32[1,16,8]{1,2,0:T(8,128)} %param.23) | copy-start | bytes 1540
  13.5 28.4 %copy-start.2 = (bf16[1,16,2048]{2,1,0:T(8,128)(2,1)S(1)}, bf16[1,16,2048]{2,1,0:T(8,128)(2,1)}, u32[]{:S(2)}) copy-start(bf16[1,16,2048]{2,1,0:T(8,128)(2,1)} %param.20) | copy-start | bytes 196612
  13.5 28.5 %copy-start.5 = (f32[2048]{0:T(1024)S(1)}, f32[2048]{0:T(1024)}, u32[]{:S(2)}) copy-start(f32[2048]{0:T(1024)} %param.22) | copy-start | bytes 24580
  87.4 1.5 copy-start.6
  87.6 1.3 copy-start.1
  88.9 1.1 copy-start.7
  97.9 4.5 %copy-start.4 = (f32[1,16,8]{1,2,0:T(8,128)S(1)}, f32[1,16,8]{1,2,0:T(8,128)}, u32[]{:S(2)}) copy-start(f32[1,16,8]{1,2,0:T(8,128)} %param.24) | copy-start | bytes 1540
  97.9 30.6 %all-to-all-start.2 = ((bf16[4,8,16,2048]{3,2,0,1:T(8,128)(2,1)}), bf16[4,8,16,2048]{3,2,0,1:T(8,128)(2,1)}, u32[]{:S(2)}, u32[]{:S(2)}) async-start(bf16[4,8,16,2048]{3,2,0,1:T(8,128)(2,1)} %copy.65), calls=%async_computation.3 | async-start | bytes 4194304 | tf_op jit(solution)/shard_map/all_to_all | solution.py:117
  102.4 45.7 %reduce-scatter.5.cloned.1.call-start = ((), (), s32[]{:S(2)}) async-start(), calls=%async_computation.6 | async-start | bytes 327680 | tf_op jit(solution)/shard_map/reduce_scatter | solution.py:126
Sparse Core Ops, SparseCore 0:
  14.8 22.1 reduce-scatter.2
  131.5 16.5 reduce-scatter.4
where the time goes:
time: 157 us; the launch traced here: 156 us
  blocking collectives  77.7 us (49%)
  waiting for transfers between devices  37.3 us (24%)
  between operations  14.4 us (9%)
  matrix products  11.3 us (7%)
  local copies, waits for them, and re-layouts  8.65 us (6%)
  starting transfers between devices  4.55 us (3%)
  other arithmetic  2.5 us (2%)
    all_to_all x1, blocking collectives, shards(): lax.all_to_all(outgoing, ('side', 'grp'), split_axis=1, concat_axis=1, ti...  29.8 us
    reduce_scatter x1, waiting for transfers between devices, shards(): lax.psum_scatter(weighted.astype(jnp.bfloat16), 'head', scatter_dimension...  16.7 us
    all_gather x1, blocking collectives, shards(): lax.all_gather(normed[None], 'head', axis=0, tiled=True)  14.5 us
    all_gather x1, blocking collectives, shards(): lax.all_gather(dispatch[None], 'head', axis=0, tiled=True)  13.5 us
    all_gather x1, blocking collectives, shards(): combine_all = lax.all_gather(combine[None], 'head', axis=0, tiled=True)  13.1 us
    all_to_all x1, waiting for transfers between devices, shards(): lax.all_to_all(partial_value, ('side', 'grp'), split_axis=1, concat_axis=...  12.7 us
    reduce_scatter x1, waiting for transfers between devices, shards(): lax.psum_scatter(halves.astype(jnp.bfloat16), 'head', scatter_dimension=1...  7.82 us
    dot_general x1, matrix products, shards(): jnp.dot(hidden, w_down[0], preferred_element_type=jnp.float32)  4.71 us
  transfers between devices with their start and end apart: 3, of which 3 were waited for; matrix products, arithmetic and copies ran while one was open for 1% of the time, Pallas kernels for 0%

commit v1 on v0

--- a/solution.py
+++ b/solution.py
@@ -3,7 +3,14 @@
 import jax
 import jax.numpy as jnp
 from jax import lax
+from jax.experimental import pallas as pl
+from jax.experimental.pallas import tpu as pltpu
 from jax.sharding import PartitionSpec as P
+
+LANES = 128
+CHUNK = 256
+MESH = pl.DeviceIdType.MESH
+NT = (((1,), (1,)), ((), ()))
 
 
 def attend(q_new, k_cache, value_cache, k_new, new_value_rows, cache_len):
@@ -52,7 +59,7 @@
     return (dispatch, combine)
 
 
-def shards(
+def shards_sparse(
     q_new,
     k_cache,
     value_cache,
@@ -129,6 +136,353 @@
     return (resid + moe_out).astype(jnp.bfloat16)[None]
 
 
+def dense_kernel(
+    q_hbm, kc_hbm, vc_hbm, kn_hbm, vn_hbm, len_ref, hid_hbm, wo_hbm, gain_hbm, ids_hbm, wts_hbm,
+    wg_hbm, wu_hbm, wd_hbm,
+    out_ref,
+    q, kc, vc, kn, vn, hid, wo, gain, ids, wts, wg, wu, wd,
+    ctx, part, part_in, resid, rows, y, y_sib, y_sum, y_in, z, z_in,
+    load_sem, ctx_send, ctx_recv, part_send, part_recv, z_send, z_recv, sib_send, sib_recv,
+    xy_send, xy_recv, fwd_send, fwd_recv, ys_send, ys_recv, yx_send, yx_recv, zo_send, zo_recv,
+):
+    side, grp, head = lax.axis_index("side"), lax.axis_index("grp"), lax.axis_index("head")
+    sides, heads = ctx.shape[0], rows.shape[2]
+    groups, rows_here, width = y.shape[0], y.shape[3], y.shape[4]
+    other = 1 - side
+
+    def group(k):
+        return lax.rem(grp // 2 + k // 2, 2) * 2 + lax.rem(lax.rem(grp, 2) + k % 2, 2)
+
+    def ahead(step):
+        return lax.rem(head + step, heads)
+
+    def behind(step):
+        return lax.rem(head + heads - step, heads)
+
+    loads = [
+        pltpu.make_async_copy(src, dst, load_sem.at[i])
+        for i, (src, dst) in enumerate(
+            [
+                (q_hbm.at[0], q), (kc_hbm.at[0, 0], kc), (kn_hbm.at[0], kn),
+                (vc_hbm.at[0, 0], vc), (vn_hbm.at[0], vn), (wo_hbm, wo), (hid_hbm.at[0], hid),
+                (gain_hbm, gain), (ids_hbm.at[0], ids), (wts_hbm.at[0], wts),
+                (wg_hbm.at[0], wg), (wu_hbm.at[0], wu), (wd_hbm.at[0], wd),
+            ]
+        )
+    ]
+    for load in loads:
+        load.start()
+
+    barrier = pltpu.get_barrier_semaphore()
+    peers = [(other, grp, head)]
+    for step in range(1, heads):
+        peers += [(side, grp, ahead(step)), (other, grp, ahead(step))]
+    peers += [(side, group(k), head) for k in range(1, groups)]
+    for peer in peers:
+        pl.semaphore_signal(barrier, inc=1, device_id=peer, device_id_type=MESH)
+
+    started = []
+
+    def send(src, dst, send_sem, recv_sem, peer):
+        copy = pltpu.make_async_remote_copy(
+            src_ref=src, dst_ref=dst, send_sem=send_sem, recv_sem=recv_sem,
+            device_id=peer, device_id_type=MESH,
+        )
+        copy.start()
+        started.append(copy)
+        return copy
+
+    new_rows, head_dim = kn.shape
+    cached = kc.shape[0]
+    per_chunk = CHUNK // head_dim
+    chunks = q.shape[1] // CHUNK
+    scale = 1.0 / math.sqrt(head_dim)
+    for load in loads[:5]:
+        load.wait()
+    valid = len_ref[0]
+    chunk_rows = per_chunk * new_rows
+    seen_cached = lax.broadcasted_iota(jnp.int32, (chunk_rows, cached), 1) < valid
+    row_pos = lax.rem(lax.broadcasted_iota(jnp.int32, (chunk_rows, new_rows), 0), new_rows)
+    seen_new = lax.broadcasted_iota(jnp.int32, (chunk_rows, new_rows), 1) <= row_pos
+    ctx_copies = []
+    for c in range(chunks):
+        queries = jnp.concatenate(
+            [q[:, c * CHUNK + j * head_dim : c * CHUNK + (j + 1) * head_dim] for j in range(per_chunk)],
+            axis=0,
+        )
+        s_old = lax.dot_general(queries, kc[...], NT, preferred_element_type=jnp.float32) * scale
+        s_new = lax.dot_general(queries, kn[...], NT, preferred_element_type=jnp.float32) * scale
+        s_old = jnp.where(seen_cached, s_old, -jnp.inf)
+        s_new = jnp.where(seen_new, s_new, -jnp.inf)
+        highest = jnp.maximum(
+            jnp.max(s_old, axis=1, keepdims=True), jnp.max(s_new, axis=1, keepdims=True)
+        )
+        e_old, e_new = jnp.exp(s_old - highest), jnp.exp(s_new - highest)
+        inverse = 1.0 / (
+            jnp.sum(e_old, axis=1, keepdims=True) + jnp.sum(e_new, axis=1, keepdims=True)
+        )
+        p_old = (e_old * inverse).astype(jnp.bfloat16)
+        p_new = (e_new * inverse).astype(jnp.bfloat16)
+        found = jnp.dot(p_old, vc[...], preferred_element_type=jnp.float32) + jnp.dot(
+            p_new, vn[...], preferred_element_type=jnp.float32
+        )
+        found = found.astype(jnp.bfloat16)
+        for j in range(per_chunk):
+            ctx[side, c, :, j * head_dim : (j + 1) * head_dim] = found[
+                j * new_rows : (j + 1) * new_rows
+            ]
+        if c == 0:
+            pl.semaphore_wait(barrier, len(peers))
+        ctx_copies.append(
+            send(
+                ctx.at[side, c], ctx.at[side, c], ctx_send.at[c], ctx_recv.at[c],
+                (other, grp, head),
+            )
+        )
+
+    for load in loads[5:10]:
+        load.wait()
+    raw = wts[...]
+    mixing = (raw / jnp.sum(raw, axis=0, keepdims=True)).astype(jnp.bfloat16).astype(jnp.float32)
+    expert = lax.broadcasted_iota(jnp.int32, (LANES, rows_here), 0)
+    table = jnp.zeros((LANES, rows_here), jnp.float32)
+    for k in range(raw.shape[0]):
+        table += jnp.where(ids[k : k + 1, :] == expert, mixing[k : k + 1, :], 0.0)
+    unit = (
+        lax.broadcasted_iota(jnp.int32, (rows_here, rows_here), 0)
+        == lax.broadcasted_iota(jnp.int32, (rows_here, rows_here), 1)
+    )
+    unit = jnp.where(unit, 1.0, 0.0).astype(jnp.bfloat16)
+    table = lax.dot_general(
+        unit, table.astype(jnp.bfloat16), NT, preferred_element_type=jnp.float32
+    )
+    rows[grp, side, head, :, width:] = table.astype(jnp.bfloat16)
+
+    for copy in ctx_copies:
+        copy.wait_recv()
+    half = wo.shape[1]
+    for n in range(0, half, CHUNK):
+        total = jnp.zeros((sides * new_rows, CHUNK), jnp.float32)
+        for c in range(chunks):
+            total += jnp.dot(
+                ctx[:, c].reshape(sides * new_rows, CHUNK),
+                wo[c * CHUNK : (c + 1) * CHUNK, n : n + CHUNK],
+                preferred_element_type=jnp.float32,
+            )
+        part[:, :, :, n : n + CHUNK] = total.astype(jnp.bfloat16).reshape(
+            sides, heads, rows_here, CHUNK
+        )
+    part_copies = []
+    for step in range(heads - 1, -1, -1):
+        for turn in range(sides):
+            if step == 0 and turn == 0:
+                continue
+            to_side = side if turn == 0 else other
+            slot = turn * heads + step
+            part_copies.append(
+                send(
+                    part.at[to_side, ahead(step)], part_in.at[side, head],
+                    part_send.at[slot], part_recv.at[slot], (to_side, grp, ahead(step)),
+                )
+            )
+    part_in[side, head] = part[side, head]
+    for copy in part_copies:
+        copy.wait_recv()
+    square = jnp.zeros((rows_here, 1), jnp.float32)
+    for piece in range(sides):
+        columns = slice(piece * half, (piece + 1) * half)
+        value = hid[:, columns].astype(jnp.float32)
+        for j in range(heads):
+            value += part_in[piece, j].astype(jnp.float32)
+        resid[:, columns] = value
+        square += jnp.sum(value * value, axis=1, keepdims=True)
+    inv_norm = lax.rsqrt(square * (1.0 / width) + 1e-06)
+    rows[grp, side, head, :, :width] = (resid[...] * inv_norm * gain[...]).astype(jnp.bfloat16)
+
+    block = rows.at[grp, side, head]
+    z_copies = [None]
+    for step in range(1, heads):
+        z_copies.append(
+            send(block, block, z_send.at[step], z_recv.at[step], (side, grp, ahead(step)))
+        )
+    sib_copies, xy_copies = [], [[] for _ in range(groups)]
+
+    def spread(step):
+        piece = rows.at[grp, side, behind(step)]
+        for k in range(1, groups):
+            xy_copies[k].append(
+                send(
+                    piece, piece, xy_send.at[k, step], xy_recv.at[k, step],
+                    (side, group(k), head),
+                )
+            )
+        sib_copies.append(
+            send(piece, piece, sib_send.at[step], sib_recv.at[step], (other, grp, head))
+        )
+
+    spread(0)
+    for step in range(1, heads):
+        z_copies[step].wait_recv()
+        spread(step)
+
+    fwd_copies, ys_copies, yx_copies = [None] * groups, [None] * groups, [None] * groups
+
+    def forward(k):
+        for copy in xy_copies[k]:
+            copy.wait_recv()
+        pieces = rows.at[group(k), side]
+        fwd_copies[k] = send(pieces, pieces, fwd_send.at[k], fwd_recv.at[k], (other, grp, head))
+
+    own_expert = side * groups + grp
+    many = sides * heads * rows_here
+
+    def experts(k):
+        at = group(k)
+        x = rows[at, :, :, :, :width].reshape(many, width)
+        gate = lax.dot_general(x, wg[...], NT, preferred_element_type=jnp.float32)
+        up = lax.dot_general(x, wu[...], NT, preferred_element_type=jnp.float32)
+        hidden = (gate / (1.0 + jnp.exp(-gate)) * up).astype(jnp.bfloat16)
+        weights = rows[at, :, :, :, width:].reshape(many, LANES).astype(jnp.float32)
+        lane = lax.broadcasted_iota(jnp.int32, (many, LANES), 1)
+        column = jnp.sum(jnp.where(lane == own_expert, weights, 0.0), axis=1, keepdims=True)
+        for n in range(0, width, 2 * CHUNK):
+            value = jnp.dot(hidden, wd[:, n : n + 2 * CHUNK], preferred_element_type=jnp.float32)
+            value = value.astype(jnp.bfloat16).astype(jnp.float32) * column
+            y[at, :, :, :, n : n + 2 * CHUNK] = value.astype(jnp.bfloat16).reshape(
+                sides, heads, rows_here, 2 * CHUNK
+            )
+        ys_copies[k] = send(
+            y.at[at, other], y_sib.at[k], ys_send.at[k], ys_recv.at[k], (other, grp, head)
+        )
+
+    def reduce_pair(k):
+        ys_copies[k].wait_recv()
+        value = y[group(k), side].astype(jnp.float32) + y_sib[k].astype(jnp.float32)
+        y_sum[k] = value.astype(jnp.bfloat16)
+        yx_copies[k] = send(
+            y_sum.at[k], y_in.at[k], yx_send.at[k], yx_recv.at[k], (side, group(k), head)
+        )
+
+    forward(1)
+    for copy in sib_copies:
+        copy.wait_recv()
+    for load in loads[10:]:
+        load.wait()
+    experts(0)
+    forward(2)
+    fwd_copies[1].wait_recv()
+    experts(1)
+    forward(3)
+    fwd_copies[2].wait_recv()
+    experts(2)
+    reduce_pair(1)
+    fwd_copies[3].wait_recv()
+    experts(3)
+    reduce_pair(2)
+    reduce_pair(3)
+    ys_copies[0].wait_recv()
+    for k in range(1, groups):
+        yx_copies[k].wait_recv()
+    for j in range(heads):
+        value = y[grp, side, j].astype(jnp.float32) + y_sib[0, j].astype(jnp.float32)
+        for k in range(1, groups):
+            value += y_in[k, j].astype(jnp.float32)
+        z[j] = value.astype(jnp.bfloat16)
+    zo_copies = []
+    for step in range(heads - 1, 0, -1):
+        zo_copies.append(
+            send(
+                z.at[ahead(step)], z_in.at[step], zo_send.at[step], zo_recv.at[step],
+                (side, grp, ahead(step)),
+            )
+        )
+    value = resid[...] + z[head].astype(jnp.float32)
+    for copy in zo_copies:
+        copy.wait_recv()
+    for step in range(1, heads):
+        value += z_in[step].astype(jnp.float32)
+    out_ref[0] = value.astype(jnp.bfloat16)
+    for copy in started:
+        copy.wait_send()
+
+
+def dense_fits(args):
+    q_new, hidden_in, expert_ids, w_down = args[0], args[6], args[9], args[13]
+    sides, groups, heads = (lax.axis_size(name) for name in ("side", "grp", "head"))
+    rows_here, top_k = expert_ids.shape[1:]
+    return (
+        2 * top_k >= sides * groups
+        and sides == 2
+        and groups == 4
+        and sides * groups <= LANES
+        and rows_here % 16 == 0
+        and q_new.shape[1] == heads * rows_here
+        and q_new.shape[2] % CHUNK == 0
+        and hidden_in.shape[2] % (2 * CHUNK) == 0
+    )
+
+
+def shards_dense(
+    q_new, k_cache, value_cache, k_new, new_value_rows, cache_len, hidden_in, out_proj, norm_gain,
+    expert_ids, gate_wts, w_gate, w_up, w_down,
+):
+    sides, groups, heads = (lax.axis_size(name) for name in ("side", "grp", "head"))
+    new_rows = q_new.shape[1]
+    rows_here, width = hidden_in.shape[1:]
+    half = out_proj.shape[1]
+    chunks = q_new.shape[2] // CHUNK
+    operands = (
+        q_new, k_cache, value_cache, k_new, new_value_rows, cache_len, hidden_in, out_proj,
+        norm_gain.reshape(1, width),
+        jnp.swapaxes(expert_ids, 1, 2), jnp.swapaxes(gate_wts, 1, 2),
+        jnp.swapaxes(w_gate, 1, 2), jnp.swapaxes(w_up, 1, 2), w_down,
+    )
+    specs = [pl.BlockSpec(memory_space=pltpu.HBM)] * len(operands)
+    specs[5] = pl.BlockSpec(memory_space=pltpu.SMEM)
+    bf16 = jnp.bfloat16
+    landed = [
+        pltpu.VMEM(operands[i].shape[cut:], operands[i].dtype)
+        for i, cut in (
+            (0, 1), (1, 2), (2, 2), (3, 1), (4, 1), (6, 1), (7, 0), (8, 0), (9, 1), (10, 1),
+            (11, 1), (12, 1), (13, 1),
+        )
+    ]
+    dma = pltpu.SemaphoreType.DMA
+    return pl.pallas_call(
+        dense_kernel,
+        out_shape=jax.ShapeDtypeStruct(hidden_in.shape, bf16),
+        in_specs=specs,
+        out_specs=pl.BlockSpec(memory_space=pltpu.VMEM),
+        scratch_shapes=landed
+        + [
+            pltpu.VMEM((sides, chunks, new_rows, CHUNK), bf16),
+            pltpu.VMEM((sides, heads, rows_here, half), bf16),
+            pltpu.VMEM((sides, heads, rows_here, half), bf16),
+            pltpu.VMEM((rows_here, width), jnp.float32),
+            pltpu.VMEM((groups, sides, heads, rows_here, width + LANES), bf16),
+            pltpu.VMEM((groups, sides, heads, rows_here, width), bf16),
+            pltpu.VMEM((groups, heads, rows_here, width), bf16),
+            pltpu.VMEM((groups, heads, rows_here, width), bf16),
+            pltpu.VMEM((groups, heads, rows_here, width), bf16),
+            pltpu.VMEM((heads, rows_here, width), bf16),
+            pltpu.VMEM((heads, rows_here, width), bf16),
+            dma((len(landed),)),
+            dma((chunks,)), dma((chunks,)),
+            dma((sides * heads,)), dma((sides * heads,)),
+            dma((heads,)), dma((heads,)),
+            dma((heads,)), dma((heads,)),
+            dma((groups, heads)), dma((groups, heads)),
+            dma((groups,)), dma((groups,)),
+            dma((groups,)), dma((groups,)),
+            dma((groups,)), dma((groups,)),
+            dma((heads,)), dma((heads,)),
+        ],
+        compiler_params=pltpu.CompilerParams(
+            collective_id=0, has_side_effects=True, vmem_limit_bytes=48 * 1024 * 1024
+        ),
+    )(*operands)
+
+
 def solution(mesh):
     in_specs = (
         P(("side", "grp"), None, "head"),
@@ -147,4 +501,9 @@
         P(("side", "grp"), "head", None),
     )
     out_specs = P(("side", "grp"), "head", None)
+    def shards(*args):
+        if dense_fits(args):
+            return shards_dense(*args)
+        return shards_sparse(*args)
+
     return jax.shard_map(shards, mesh=mesh, in_specs=in_specs, out_specs=out_specs, check_vma=False)

time: 157 us -> 70.9 us (0.45)
  blocking collectives: 77.7 us -> 0 us
  Pallas kernels: 0 us -> 56.9 us
  waiting for transfers between devices: 37.3 us -> 0 us
  between operations: 14.4 us -> 0.68 us
  matrix products: 11.3 us -> 0 us
  starting transfers between devices: 4.55 us -> 0 us
  local copies, waits for them, and re-layouts: 8.65 us -> 12.7 us
  other arithmetic: 2.5 us -> 0 us
    pallas_call x0 -> x1, Pallas kernels: none -> 56.9 us  [shards_dense(): pl.pallas_call(dense_kernel, out_shape=jax.ShapeDtypeStruct(hidden_in.sha...]
    all_gather x4 -> x0, blocking collectives: 43.1 us -> none  [the longest x1 14.5 us: shards(): lax.all_gather(normed[None], 'head', axis=0, tiled=True)]
    all_to_all x2 -> x0, blocking collectives: 34.5 us -> none  [the longest x1 29.8 us: shards(): lax.all_to_all(outgoing, ('side', 'grp'), split_axis=1, concat_axis=1, ti...]
    reduce_scatter x2 -> x0, waiting for transfers between devices: 24.6 us -> none  [the longest x1 16.7 us: shards(): lax.psum_scatter(weighted.astype(jnp.bfloat16), 'head', scatter_dimension...]
    all_to_all x1 -> x0, waiting for transfers between devices: 12.7 us -> none  [shards(): lax.all_to_all(partial_value, ('side', 'grp'), split_axis=1, concat_axis=...]
    unnamed x27, local copies, waits for them, and re-layouts: 2.66 us -> 12.7 us
    dot_general x6 -> x0, matrix products: 9.73 us -> none  [the longest x1 4.71 us: shards(): jnp.dot(hidden, w_down[0], preferred_element_type=jnp.float32)]
    all_to_all x1 -> x0, starting transfers between devices: 4.47 us -> none  [shards(): lax.all_to_all(partial_value, ('side', 'grp'), split_axis=1, concat_axis=...]
  transfers between devices with their start and end apart: 3 -> 0, of which waited for: 3 -> 0; matrix products, arithmetic and copies ran while one was open for 1% -> 0% of each run, Pallas kernels for 0% -> 0%
where the time goes in v1:
time: 70.9 us; the launch traced here: 70.3 us
  Pallas kernels  56.9 us (80%)
  local copies, waits for them, and re-layouts  12.7 us (18%)
    pallas_call x1, Pallas kernels, shards_dense(): pl.pallas_call(dense_kernel, out_shape=jax.ShapeDtypeStruct(hidden_in.sha...  56.9 us
    unnamed x27, local copies, waits for them, and re-layouts  12.7 us

profile of v1, /device:TPU:0, one launch (start us, length us, event | category | flops | bytes accessed | tf_op | source)
XLA Modules:
  0.0 70.3 jit_solution(4931170023255826773)
XLA Ops:
  0.7 0.0 copy-start
  0.7 1.6 %copy-done = bf16[1024,1024]{1,0:T(8,128)(2,1)S(1)} copy-done((bf16[1024,1024]{1,0:T(8,128)(2,1)S(1)}, bf16[1024,1024]{1,0:T(8,128)(2,1)}, u32[]{:S(2)}) %copy-start) | copy-done | bytes 2097176
  2.2 0.0 copy-start.1
  2.2 1.1 %copy-done.1 = bf16[1,2048,192]{1,2,0:T(8,128)(2,1)S(1)} copy-done((bf16[1,2048,192]{1,2,0:T(8,128)(2,1)S(1)}, bf16[1,2048,192]{1,2,0:T(8,128)(2,1)}, u32[]{:S(2)}) %copy-start.1) | copy-done | bytes 786456
  3.4 0.0 copy-start.2
  3.4 1.1 %copy-done.2 = bf16[1,2048,192]{1,2,0:T(8,128)(2,1)S(1)} copy-done((bf16[1,2048,192]{1,2,0:T(8,128)(2,1)S(1)}, bf16[1,2048,192]{1,2,0:T(8,128)(2,1)}, u32[]{:S(2)}) %copy-start.2) | copy-done | bytes 786456
  4.5 0.0 copy-start.3
  4.5 1.1 %copy-done.3 = bf16[1,192,2048]{2,1,0:T(8,128)(2,1)S(1)} copy-done((bf16[1,192,2048]{2,1,0:T(8,128)(2,1)S(1)}, bf16[1,192,2048]{2,1,0:T(8,128)(2,1)}, u32[]{:S(2)}) %copy-start.3) | copy-done | bytes 786456
  5.6 0.0 copy-start.4
  5.6 0.9 %copy-done.4 = bf16[1,64,1024]{2,1,0:T(8,128)(2,1)S(1)} copy-done((bf16[1,64,1024]{2,1,0:T(8,128)(2,1)S(1)}, bf16[1,64,1024]{2,1,0:T(8,128)(2,1)}, u32[]{:S(2)}) %copy-start.4) | copy-done | bytes 131096
  6.6 0.0 copy-start.5
  6.6 0.9 %copy-done.5 = bf16[1,1,512,128]{3,2,1,0:T(8,128)(2,1)S(1)} copy-done((bf16[1,1,512,128]{3,2,1,0:T(8,128)(2,1)S(1)}, bf16[1,1,512,128]{3,2,1,0:T(8,128)(2,1)}, u32[]{:S(2)}) %copy-start.5) | copy-done | bytes 131096
  7.5 0.0 copy-start.6
  7.5 0.9 %copy-done.6 = bf16[1,1,512,128]{3,2,1,0:T(8,128)(2,1)S(1)} copy-done((bf16[1,1,512,128]{3,2,1,0:T(8,128)(2,1)S(1)}, bf16[1,1,512,128]{3,2,1,0:T(8,128)(2,1)}, u32[]{:S(2)}) %copy-start.6) | copy-done | bytes 131096
  8.4 0.0 copy-start.7
  8.4 0.8 %copy-done.7 = bf16[1,16,2048]{2,1,0:T(8,128)(2,1)S(1)} copy-done((bf16[1,16,2048]{2,1,0:T(8,128)(2,1)S(1)}, bf16[1,16,2048]{2,1,0:T(8,128)(2,1)}, u32[]{:S(2)}) %copy-start.7) | copy-done | bytes 65560
  9.2 0.0 copy-start.8
  9.2 0.7 %copy-done.8 = bf16[1,64,128]{2,1,0:T(8,128)(2,1)S(1)} copy-done((bf16[1,64,128]{2,1,0:T(8,128)(2,1)S(1)}, bf16[1,64,128]{2,1,0:T(8,128)(2,1)}, u32[]{:S(2)}) %copy-start.8) | copy-done | bytes 16408
  9.9 0.0 copy-start.9
  9.9 0.7 %copy-done.9 = bf16[1,64,128]{2,1,0:T(8,128)(2,1)S(1)} copy-done((bf16[1,64,128]{2,1,0:T(8,128)(2,1)S(1)}, bf16[1,64,128]{2,1,0:T(8,128)(2,1)}, u32[]{:S(2)}) %copy-start.9) | copy-done | bytes 16408
  10.6 0.0 copy-start.10
  10.6 0.7 copy-done.10
  11.3 0.0 copy-start.11
  11.3 0.7 copy-done.11
  12.0 0.0 copy-start.12
  12.0 0.7 copy-done.12
  12.7 56.9 %shard_map.136 = bf16[1,16,2048]{2,1,0:T(8,128)(2,1)S(1)} custom-call(bf16[1,64,1024]{2,1,0:T(8,128)(2,1)S(1)} %copy-done.4, bf16[1,1,512,128]{3,2,1,0:T(8,128)(2,1)S(1)} %copy-done.5, bf16[1,1,512,128]{3,2,1,0:T(8,128)(2,1)S(1)} %copy-done.6, bf16[1,64,128]{2,1,0:T(8,128)(2,1)S(1)} %copy-done.8, bf16[1,64,128]{2,1,0:T(8,128)(2,1)S(1)} %copy-done.9, ...), custom_call_target="tpu_custom_call" | custom-call | tf_op jit(solution)/shard_map/pallas_call | solution.py:451
  69.6 0.6 copy.17
Async XLA Ops:
  0.7 1.6 %copy-start = (bf16[1024,1024]{1,0:T(8,128)(2,1)S(1)}, bf16[1024,1024]{1,0:T(8,128)(2,1)}, u32[]{:S(2)}) copy-start(bf16[1024,1024]{1,0:T(8,128)(2,1)} %wo_hbm.1) | copy-start | bytes 6291460
  2.2 1.1 %copy-start.1 = (bf16[1,2048,192]{1,2,0:T(8,128)(2,1)S(1)}, bf16[1,2048,192]{1,2,0:T(8,128)(2,1)}, u32[]{:S(2)}) copy-start(bf16[1,2048,192]{1,2,0:T(8,128)(2,1)} %param.25) | copy-start | bytes 2359300
  3.4 1.1 %copy-start.2 = (bf16[1,2048,192]{1,2,0:T(8,128)(2,1)S(1)}, bf16[1,2048,192]{1,2,0:T(8,128)(2,1)}, u32[]{:S(2)}) copy-start(bf16[1,2048,192]{1,2,0:T(8,128)(2,1)} %param.26) | copy-start | bytes 2359300
  4.5 1.1 %copy-start.3 = (bf16[1,192,2048]{2,1,0:T(8,128)(2,1)S(1)}, bf16[1,192,2048]{2,1,0:T(8,128)(2,1)}, u32[]{:S(2)}) copy-start(bf16[1,192,2048]{2,1,0:T(8,128)(2,1)} %wd_hbm.1) | copy-start | bytes 2359300
  5.6 0.9 %copy-start.4 = (bf16[1,64,1024]{2,1,0:T(8,128)(2,1)S(1)}, bf16[1,64,1024]{2,1,0:T(8,128)(2,1)}, u32[]{:S(2)}) copy-start(bf16[1,64,1024]{2,1,0:T(8,128)(2,1)} %q_hbm.1) | copy-start | bytes 393220
  6.6 0.9 %copy-start.5 = (bf16[1,1,512,128]{3,2,1,0:T(8,128)(2,1)S(1)}, bf16[1,1,512,128]{3,2,1,0:T(8,128)(2,1)}, u32[]{:S(2)}) copy-start(bf16[1,1,512,128]{3,2,1,0:T(8,128)(2,1)} %kc_hbm.1) | copy-start | bytes 393220
  7.5 0.9 %copy-start.6 = (bf16[1,1,512,128]{3,2,1,0:T(8,128)(2,1)S(1)}, bf16[1,1,512,128]{3,2,1,0:T(8,128)(2,1)}, u32[]{:S(2)}) copy-start(bf16[1,1,512,128]{3,2,1,0:T(8,128)(2,1)} %vc_hbm.1) | copy-start | bytes 393220
  8.4 0.8 %copy-start.7 = (bf16[1,16,2048]{2,1,0:T(8,128)(2,1)S(1)}, bf16[1,16,2048]{2,1,0:T(8,128)(2,1)}, u32[]{:S(2)}) copy-start(bf16[1,16,2048]{2,1,0:T(8,128)(2,1)} %hid_hbm.1) | copy-start | bytes 196612
  9.2 0.7 %copy-start.8 = (bf16[1,64,128]{2,1,0:T(8,128)(2,1)S(1)}, bf16[1,64,128]{2,1,0:T(8,128)(2,1)}, u32[]{:S(2)}) copy-start(bf16[1,64,128]{2,1,0:T(8,128)(2,1)} %kn_hbm.1) | copy-start | bytes 49156
  9.9 0.7 %copy-start.9 = (bf16[1,64,128]{2,1,0:T(8,128)(2,1)S(1)}, bf16[1,64,128]{2,1,0:T(8,128)(2,1)}, u32[]{:S(2)}) copy-start(bf16[1,64,128]{2,1,0:T(8,128)(2,1)} %vn_hbm.1) | copy-start | bytes 49156
  10.6 0.7 copy-start.10
  11.3 0.7 copy-start.11
  12.0 0.7 copy-start.12

commit v2 on v1

--- a/solution.py
+++ b/solution.py
@@ -141,13 +141,12 @@
     wg_hbm, wu_hbm, wd_hbm,
     out_ref,
     q, kc, vc, kn, vn, hid, wo, gain, ids, wts, wg, wu, wd,
-    ctx, part, part_in, resid, rows, y, y_sib, y_sum, y_in, z, z_in,
+    ctx, part, part_in, resid, rows, y, y_sib, y_sum, y_a, y_fwd, y_b, z, z_in,
     load_sem, ctx_send, ctx_recv, part_send, part_recv, z_send, z_recv, sib_send, sib_recv,
-    xy_send, xy_recv, fwd_send, fwd_recv, ys_send, ys_recv, yx_send, yx_recv, zo_send, zo_recv,
+    xy_send, xy_recv, ys_send, ys_recv, ya_send, ya_recv, yb_send, yb_recv, zo_send, zo_recv,
 ):
     side, grp, head = lax.axis_index("side"), lax.axis_index("grp"), lax.axis_index("head")
-    sides, heads = ctx.shape[0], rows.shape[2]
-    groups, rows_here, width = y.shape[0], y.shape[3], y.shape[4]
+    heads, sides, groups, rows_here, width = y.shape
     other = 1 - side
 
     def group(k):
@@ -177,7 +176,7 @@
     peers = [(other, grp, head)]
     for step in range(1, heads):
         peers += [(side, grp, ahead(step)), (other, grp, ahead(step))]
-    peers += [(side, group(k), head) for k in range(1, groups)]
+    peers += [(side, group(1), head), (side, group(2), head)]
     for peer in peers:
         pl.semaphore_signal(barrier, inc=1, device_id=peer, device_id_type=MESH)
 
@@ -256,7 +255,7 @@
     table = lax.dot_general(
         unit, table.astype(jnp.bfloat16), NT, preferred_element_type=jnp.float32
     )
-    rows[grp, side, head, :, width:] = table.astype(jnp.bfloat16)
+    rows[head, side, grp, :, width:] = table.astype(jnp.bfloat16)
 
     for copy in ctx_copies:
         copy.wait_recv()
@@ -297,47 +296,59 @@
         resid[:, columns] = value
         square += jnp.sum(value * value, axis=1, keepdims=True)
     inv_norm = lax.rsqrt(square * (1.0 / width) + 1e-06)
-    rows[grp, side, head, :, :width] = (resid[...] * inv_norm * gain[...]).astype(jnp.bfloat16)
-
-    block = rows.at[grp, side, head]
-    z_copies = [None]
-    for step in range(1, heads):
-        z_copies.append(
-            send(block, block, z_send.at[step], z_recv.at[step], (side, grp, ahead(step)))
-        )
-    sib_copies, xy_copies = [], [[] for _ in range(groups)]
+    rows[head, side, grp, :, :width] = (resid[...] * inv_norm * gain[...]).astype(jnp.bfloat16)
+
+    z_copies, sib_copies = [None] * heads, [[] for _ in range(heads)]
+    xy_copies = [[None] * groups for _ in range(heads)]
+    ys_copies, ya_copies, yb_copies = [None] * heads, [None] * heads, [None] * heads
+    zo_copies = []
+    own_expert = side * groups + grp
+    many = sides * groups * rows_here
+
+    def axes(step):
+        return (1, 2) if step % 2 == 0 else (2, 1)
+
+    def to_group(step, k, origin):
+        piece = rows.at[behind(step), side, group(origin)]
+        slot = k if origin == 0 else origin ^ k
+        xy_copies[step][slot] = send(
+            piece, piece, xy_send.at[step, slot], xy_recv.at[step, slot], (side, group(k), head)
+        )
+
+    def to_core(step, origin):
+        piece = rows.at[behind(step), side, group(origin)]
+        sib_copies[step].append(
+            send(
+                piece, piece, sib_send.at[step, origin], sib_recv.at[step, origin],
+                (other, grp, head),
+            )
+        )
 
     def spread(step):
-        piece = rows.at[grp, side, behind(step)]
-        for k in range(1, groups):
-            xy_copies[k].append(
-                send(
-                    piece, piece, xy_send.at[k, step], xy_recv.at[k, step],
-                    (side, group(k), head),
-                )
-            )
-        sib_copies.append(
-            send(piece, piece, sib_send.at[step], sib_recv.at[step], (other, grp, head))
-        )
-
-    spread(0)
-    for step in range(1, heads):
-        z_copies[step].wait_recv()
-        spread(step)
-
-    fwd_copies, ys_copies, yx_copies = [None] * groups, [None] * groups, [None] * groups
-
-    def forward(k):
-        for copy in xy_copies[k]:
+        if step > 0:
+            z_copies[step].wait_recv()
+        first, second = axes(step)
+        to_group(step, first, 0)
+        to_group(step, second, 0)
+        to_core(step, 0)
+
+    def relay(step):
+        first, second = axes(step)
+        xy_copies[step][first].wait_recv()
+        to_group(step, second, first)
+        to_core(step, first)
+        xy_copies[step][second].wait_recv()
+        to_core(step, second)
+        xy_copies[step][3].wait_recv()
+        to_core(step, 3)
+
+    def experts(step):
+        at = behind(step)
+        if step == 0:
+            for load in loads[10:]:
+                load.wait()
+        for copy in sib_copies[step]:
             copy.wait_recv()
-        pieces = rows.at[group(k), side]
-        fwd_copies[k] = send(pieces, pieces, fwd_send.at[k], fwd_recv.at[k], (other, grp, head))
-
-    own_expert = side * groups + grp
-    many = sides * heads * rows_here
-
-    def experts(k):
-        at = group(k)
         x = rows[at, :, :, :, :width].reshape(many, width)
         gate = lax.dot_general(x, wg[...], NT, preferred_element_type=jnp.float32)
         up = lax.dot_general(x, wu[...], NT, preferred_element_type=jnp.float32)
@@ -349,57 +360,69 @@
             value = jnp.dot(hidden, wd[:, n : n + 2 * CHUNK], preferred_element_type=jnp.float32)
             value = value.astype(jnp.bfloat16).astype(jnp.float32) * column
             y[at, :, :, :, n : n + 2 * CHUNK] = value.astype(jnp.bfloat16).reshape(
-                sides, heads, rows_here, 2 * CHUNK
-            )
-        ys_copies[k] = send(
-            y.at[at, other], y_sib.at[k], ys_send.at[k], ys_recv.at[k], (other, grp, head)
-        )
-
-    def reduce_pair(k):
-        ys_copies[k].wait_recv()
-        value = y[group(k), side].astype(jnp.float32) + y_sib[k].astype(jnp.float32)
-        y_sum[k] = value.astype(jnp.bfloat16)
-        yx_copies[k] = send(
-            y_sum.at[k], y_in.at[k], yx_send.at[k], yx_recv.at[k], (side, group(k), head)
-        )
-
-    forward(1)
-    for copy in sib_copies:
-        copy.wait_recv()
-    for load in loads[10:]:
-        load.wait()
-    experts(0)
-    forward(2)
-    fwd_copies[1].wait_recv()
-    experts(1)
-    forward(3)
-    fwd_copies[2].wait_recv()
-    experts(2)
-    reduce_pair(1)
-    fwd_copies[3].wait_recv()
-    experts(3)
-    reduce_pair(2)
-    reduce_pair(3)
-    ys_copies[0].wait_recv()
-    for k in range(1, groups):
-        yx_copies[k].wait_recv()
-    for j in range(heads):
-        value = y[grp, side, j].astype(jnp.float32) + y_sib[0, j].astype(jnp.float32)
-        for k in range(1, groups):
-            value += y_in[k, j].astype(jnp.float32)
-        z[j] = value.astype(jnp.bfloat16)
-    zo_copies = []
-    for step in range(heads - 1, 0, -1):
-        zo_copies.append(
+                sides, groups, rows_here, 2 * CHUNK
+            )
+        ys_copies[step] = send(
+            y.at[at, other], y_sib.at[step], ys_send.at[step], ys_recv.at[step],
+            (other, grp, head),
+        )
+
+    def reduce_cores(step):
+        ys_copies[step].wait_recv()
+        value = y[behind(step), side].astype(jnp.float32) + y_sib[step].astype(jnp.float32)
+        y_sum[step] = value.astype(jnp.bfloat16)
+        first, _ = axes(step)
+        peer = (side, group(first), head)
+        ya_copies[step] = [
             send(
-                z.at[ahead(step)], z_in.at[step], zo_send.at[step], zo_recv.at[step],
-                (side, grp, ahead(step)),
-            )
-        )
-    value = resid[...] + z[head].astype(jnp.float32)
-    for copy in zo_copies:
-        copy.wait_recv()
+                y_sum.at[step, group(k)], y_a.at[step, i], ya_send.at[step, i],
+                ya_recv.at[step, i], peer,
+            )
+            for i, k in enumerate((3, first))
+        ]
+
+    def reduce_first(step):
+        ya_copies[step][0].wait_recv()
+        _, second = axes(step)
+        value = y_sum[step, group(second)].astype(jnp.float32) + y_a[step, 0].astype(jnp.float32)
+        y_fwd[step] = value.astype(jnp.bfloat16)
+        yb_copies[step] = send(
+            y_fwd.at[step], y_b.at[step], yb_send.at[step], yb_recv.at[step],
+            (side, group(second), head),
+        )
+
+    def reduce_second(step):
+        ya_copies[step][1].wait_recv()
+        yb_copies[step].wait_recv()
+        value = y_sum[step, grp].astype(jnp.float32) + y_a[step, 1].astype(jnp.float32)
+        value += y_b[step].astype(jnp.float32)
+        if step == 0:
+            resid[...] += value
+        else:
+            z[step] = value.astype(jnp.bfloat16)
+            zo_copies.append(
+                send(
+                    z.at[step], z_in.at[step], zo_send.at[step], zo_recv.at[step],
+                    (side, grp, behind(step)),
+                )
+            )
+
+    block = rows.at[head, side, grp]
     for step in range(1, heads):
+        z_copies[step] = send(
+            block, block, z_send.at[step], z_recv.at[step], (side, grp, ahead(step))
+        )
+    later = (reduce_second, reduce_first, reduce_cores, experts, relay)
+    for tick in range(heads + len(later)):
+        if tick < heads:
+            spread(tick)
+        for i, stage in enumerate(later):
+            step = tick - len(later) + i
+            if 0 <= step < heads:
+                stage(step)
+    value = resid[...]
+    for step in range(1, heads):
+        zo_copies[step - 1].wait_recv()
         value += z_in[step].astype(jnp.float32)
     out_ref[0] = value.astype(jnp.bfloat16)
     for copy in started:
@@ -459,26 +482,28 @@
             pltpu.VMEM((sides, heads, rows_here, half), bf16),
             pltpu.VMEM((sides, heads, rows_here, half), bf16),
             pltpu.VMEM((rows_here, width), jnp.float32),
-            pltpu.VMEM((groups, sides, heads, rows_here, width + LANES), bf16),
-            pltpu.VMEM((groups, sides, heads, rows_here, width), bf16),
-            pltpu.VMEM((groups, heads, rows_here, width), bf16),
-            pltpu.VMEM((groups, heads, rows_here, width), bf16),
-            pltpu.VMEM((groups, heads, rows_here, width), bf16),
+            pltpu.VMEM((heads, sides, groups, rows_here, width + LANES), bf16),
+            pltpu.VMEM((heads, sides, groups, rows_here, width), bf16),
+            pltpu.VMEM((heads, groups, rows_here, width), bf16),
+            pltpu.VMEM((heads, groups, rows_here, width), bf16),
+            pltpu.VMEM((heads, 2, rows_here, width), bf16),
+            pltpu.VMEM((heads, rows_here, width), bf16),
+            pltpu.VMEM((heads, rows_here, width), bf16),
             pltpu.VMEM((heads, rows_here, width), bf16),
             pltpu.VMEM((heads, rows_here, width), bf16),
             dma((len(landed),)),
             dma((chunks,)), dma((chunks,)),
             dma((sides * heads,)), dma((sides * heads,)),
             dma((heads,)), dma((heads,)),
+            dma((heads, groups)), dma((heads, groups)),
+            dma((heads, groups)), dma((heads, groups)),
             dma((heads,)), dma((heads,)),
-            dma((groups, heads)), dma((groups, heads)),
-            dma((groups,)), dma((groups,)),
-            dma((groups,)), dma((groups,)),
-            dma((groups,)), dma((groups,)),
+            dma((heads, 2)), dma((heads, 2)),
+            dma((heads,)), dma((heads,)),
             dma((heads,)), dma((heads,)),
         ],
         compiler_params=pltpu.CompilerParams(
-            collective_id=0, has_side_effects=True, vmem_limit_bytes=48 * 1024 * 1024
+            collective_id=0, has_side_effects=True, vmem_limit_bytes=60 * 1024 * 1024
         ),
     )(*operands)
 

time: 70.9 us -> 62.4 us (0.88)
  local copies, waits for them, and re-layouts: 12.7 us -> 1.47 us
  Pallas kernels: 56.9 us -> 60.1 us
    unnamed x27 -> x1, local copies, waits for them, and re-layouts: 12.7 us -> 1.47 us
    pallas_call x1, Pallas kernels: 56.9 us -> 60.1 us  [shards_dense(): pl.pallas_call(dense_kernel, out_shape=jax.ShapeDtypeStruct(hidden_in.sha...]
where the time goes in v2:
time: 62.4 us; the launch traced here: 62.3 us
  Pallas kernels  60.1 us (96%)
  local copies, waits for them, and re-layouts  1.47 us (2%)
  between operations  0.66 us (1%)
    pallas_call x1, Pallas kernels, shards_dense(): pl.pallas_call(dense_kernel, out_shape=jax.ShapeDtypeStruct(hidden_in.sha...  60.1 us
    unnamed x1, local copies, waits for them, and re-layouts  1.47 us

profile of v2, /device:TPU:0, one launch (start us, length us, event | category | flops | bytes accessed | tf_op | source)
XLA Modules:
  0.0 62.3 jit_solution(2603489003950670987)
XLA Ops:
  0.7 60.1 %shard_map.136 = bf16[1,16,2048]{2,1,0:T(8,128)(2,1)} custom-call(bf16[1,64,1024]{2,1,0:T(8,128)(2,1)} %q_hbm.1, bf16[1,1,512,128]{3,2,1,0:T(8,128)(2,1)} %kc_hbm.1, bf16[1,1,512,128]{3,2,1,0:T(8,128)(2,1)} %vc_hbm.1, bf16[1,64,128]{2,1,0:T(8,128)(2,1)} %kn_hbm.1, bf16[1,64,128]{2,1,0:T(8,128)(2,1)} %vn_hbm.1, s32[1]{0:T(128)S(6)} %copy.16.len_ref, ...), custom_call_target="tpu_custom_call" | custom-call | tf_op jit(solution)/shard_map/pallas_call | solution.py:474
  60.8 1.5 %copy.17 = bf16[1,16,2048]{2,1,0:T(8,128)(2,1)} copy(bf16[1,16,2048]{2,1,0:T(8,128)(2,1)} %shard_map.136) | data formatting | bytes 131072

commit v3 on v2

--- a/solution.py
+++ b/solution.py
@@ -169,14 +169,14 @@
             ]
         )
     ]
-    for load in loads:
+    for load in loads[:5]:
         load.start()
 
     barrier = pltpu.get_barrier_semaphore()
     peers = [(other, grp, head)]
     for step in range(1, heads):
         peers += [(side, grp, ahead(step)), (other, grp, ahead(step))]
-    peers += [(side, group(1), head), (side, group(2), head)]
+    peers += [(side, group(k), head) for k in range(1, groups)]
     for peer in peers:
         pl.semaphore_signal(barrier, inc=1, device_id=peer, device_id_type=MESH)
 
@@ -191,28 +191,35 @@
         started.append(copy)
         return copy
 
-    new_rows, head_dim = kn.shape
-    cached = kc.shape[0]
-    per_chunk = CHUNK // head_dim
-    chunks = q.shape[1] // CHUNK
+    head_dim = kn.shape[1]
+    new_rows, cached = kn.shape[0], kc.shape[0]
+    query_groups = q.shape[1] // head_dim
+    half = wo.shape[1]
     scale = 1.0 / math.sqrt(head_dim)
     for load in loads[:5]:
         load.wait()
+    for load in loads[5:]:
+        load.start()
     valid = len_ref[0]
-    chunk_rows = per_chunk * new_rows
-    seen_cached = lax.broadcasted_iota(jnp.int32, (chunk_rows, cached), 1) < valid
-    row_pos = lax.rem(lax.broadcasted_iota(jnp.int32, (chunk_rows, new_rows), 0), new_rows)
-    seen_new = lax.broadcasted_iota(jnp.int32, (chunk_rows, new_rows), 1) <= row_pos
-    ctx_copies = []
-    for c in range(chunks):
+    many_queries = query_groups * rows_here
+    seen_cached = lax.broadcasted_iota(jnp.int32, (many_queries, cached), 1) < valid
+    row_pos = lax.rem(lax.broadcasted_iota(jnp.int32, (many_queries, new_rows), 0), rows_here)
+    new_pos = lax.broadcasted_iota(jnp.int32, (many_queries, new_rows), 1) - row_pos
+    ctx_copies, part_copies = [None] * heads, []
+
+    def attend_rows(step):
+        start = pl.multiple_of(ahead(step) * rows_here, rows_here)
         queries = jnp.concatenate(
-            [q[:, c * CHUNK + j * head_dim : c * CHUNK + (j + 1) * head_dim] for j in range(per_chunk)],
+            [
+                q[pl.ds(start, rows_here), j * head_dim : (j + 1) * head_dim]
+                for j in range(query_groups)
+            ],
             axis=0,
         )
         s_old = lax.dot_general(queries, kc[...], NT, preferred_element_type=jnp.float32) * scale
         s_new = lax.dot_general(queries, kn[...], NT, preferred_element_type=jnp.float32) * scale
         s_old = jnp.where(seen_cached, s_old, -jnp.inf)
-        s_new = jnp.where(seen_new, s_new, -jnp.inf)
+        s_new = jnp.where(new_pos <= start, s_new, -jnp.inf)
         highest = jnp.maximum(
             jnp.max(s_old, axis=1, keepdims=True), jnp.max(s_new, axis=1, keepdims=True)
         )
@@ -226,20 +233,46 @@
             p_new, vn[...], preferred_element_type=jnp.float32
         )
         found = found.astype(jnp.bfloat16)
-        for j in range(per_chunk):
-            ctx[side, c, :, j * head_dim : (j + 1) * head_dim] = found[
-                j * new_rows : (j + 1) * new_rows
+        for j in range(query_groups):
+            ctx[side, step, :, j * head_dim : (j + 1) * head_dim] = found[
+                j * rows_here : (j + 1) * rows_here
             ]
-        if c == 0:
+        if step == heads - 1:
             pl.semaphore_wait(barrier, len(peers))
-        ctx_copies.append(
-            send(
-                ctx.at[side, c], ctx.at[side, c], ctx_send.at[c], ctx_recv.at[c],
-                (other, grp, head),
-            )
-        )
-
-    for load in loads[5:10]:
+        ctx_copies[step] = send(
+            ctx.at[side, step], ctx.at[side, step], ctx_send.at[step], ctx_recv.at[step],
+            (other, grp, head),
+        )
+
+    def project_rows(step):
+        if step == heads - 1:
+            loads[5].wait()
+        ctx_copies[step].wait_recv()
+        both = ctx[:, step].reshape(sides * rows_here, ctx.shape[3])
+        for n in range(0, half, CHUNK):
+            total = jnp.dot(both, wo[:, n : n + CHUNK], preferred_element_type=jnp.float32)
+            part[:, step, :, n : n + CHUNK] = total.astype(jnp.bfloat16).reshape(
+                sides, rows_here, CHUNK
+            )
+        for turn, to_side in enumerate((side, other)):
+            if step == 0 and turn == 0:
+                part_in[side, head] = part[side, 0]
+                continue
+            slot = turn * heads + step
+            part_copies.append(
+                send(
+                    part.at[to_side, step], part_in.at[side, head],
+                    part_send.at[slot], part_recv.at[slot], (to_side, grp, ahead(step)),
+                )
+            )
+
+    attend_rows(heads - 1)
+    for step in range(heads - 2, -1, -1):
+        attend_rows(step)
+        project_rows(step + 1)
+    project_rows(0)
+
+    for load in loads[6:10]:
         load.wait()
     raw = wts[...]
     mixing = (raw / jnp.sum(raw, axis=0, keepdims=True)).astype(jnp.bfloat16).astype(jnp.float32)
@@ -257,34 +290,6 @@
     )
     rows[head, side, grp, :, width:] = table.astype(jnp.bfloat16)
 
-    for copy in ctx_copies:
-        copy.wait_recv()
-    half = wo.shape[1]
-    for n in range(0, half, CHUNK):
-        total = jnp.zeros((sides * new_rows, CHUNK), jnp.float32)
-        for c in range(chunks):
-            total += jnp.dot(
-                ctx[:, c].reshape(sides * new_rows, CHUNK),
-                wo[c * CHUNK : (c + 1) * CHUNK, n : n + CHUNK],
-                preferred_element_type=jnp.float32,
-            )
-        part[:, :, :, n : n + CHUNK] = total.astype(jnp.bfloat16).reshape(
-            sides, heads, rows_here, CHUNK
-        )
-    part_copies = []
-    for step in range(heads - 1, -1, -1):
-        for turn in range(sides):
-            if step == 0 and turn == 0:
-                continue
-            to_side = side if turn == 0 else other
-            slot = turn * heads + step
-            part_copies.append(
-                send(
-                    part.at[to_side, ahead(step)], part_in.at[side, head],
-                    part_send.at[slot], part_recv.at[slot], (to_side, grp, ahead(step)),
-                )
-            )
-    part_in[side, head] = part[side, head]
     for copy in part_copies:
         copy.wait_recv()
     square = jnp.zeros((rows_here, 1), jnp.float32)
@@ -324,10 +329,15 @@
             )
         )
 
+    def relayed(step):
+        return step < heads - 1
+
     def spread(step):
         if step > 0:
             z_copies[step].wait_recv()
         first, second = axes(step)
+        if not relayed(step):
+            to_group(step, 3, 0)
         to_group(step, first, 0)
         to_group(step, second, 0)
         to_core(step, 0)
@@ -335,10 +345,13 @@
     def relay(step):
         first, second = axes(step)
         xy_copies[step][first].wait_recv()
-        to_group(step, second, first)
+        if relayed(step):
+            to_group(step, second, first)
         to_core(step, first)
         xy_copies[step][second].wait_recv()
         to_core(step, second)
+
+    def finish(step):
         xy_copies[step][3].wait_recv()
         to_core(step, 3)
 
@@ -371,18 +384,24 @@
         ys_copies[step].wait_recv()
         value = y[behind(step), side].astype(jnp.float32) + y_sib[step].astype(jnp.float32)
         y_sum[step] = value.astype(jnp.bfloat16)
-        first, _ = axes(step)
-        peer = (side, group(first), head)
+        first, second = axes(step)
         ya_copies[step] = [
             send(
                 y_sum.at[step, group(k)], y_a.at[step, i], ya_send.at[step, i],
-                ya_recv.at[step, i], peer,
+                ya_recv.at[step, i], (side, group(first if relayed(step) else k), head),
             )
             for i, k in enumerate((3, first))
         ]
+        if not relayed(step):
+            yb_copies[step] = send(
+                y_sum.at[step, group(second)], y_b.at[step], yb_send.at[step],
+                yb_recv.at[step], (side, group(second), head),
+            )
 
     def reduce_first(step):
         ya_copies[step][0].wait_recv()
+        if not relayed(step):
+            return
         _, second = axes(step)
         value = y_sum[step, group(second)].astype(jnp.float32) + y_a[step, 0].astype(jnp.float32)
         y_fwd[step] = value.astype(jnp.bfloat16)
@@ -396,6 +415,8 @@
         yb_copies[step].wait_recv()
         value = y_sum[step, grp].astype(jnp.float32) + y_a[step, 1].astype(jnp.float32)
         value += y_b[step].astype(jnp.float32)
+        if not relayed(step):
+            value += y_a[step, 0].astype(jnp.float32)
         if step == 0:
             resid[...] += value
         else:
@@ -412,14 +433,16 @@
         z_copies[step] = send(
             block, block, z_send.at[step], z_recv.at[step], (side, grp, ahead(step))
         )
-    later = (reduce_second, reduce_first, reduce_cores, experts, relay)
-    for tick in range(heads + len(later)):
-        if tick < heads:
-            spread(tick)
-        for i, stage in enumerate(later):
-            step = tick - len(later) + i
-            if 0 <= step < heads:
-                stage(step)
+    stages = (
+        (0, spread), (2, relay), (4, finish), (6, experts), (9, reduce_cores),
+        (11, reduce_first), (13, reduce_second),
+    )
+    for _, _, stage, step in sorted(
+        (delay + 2 * step, delay, stage, step)
+        for delay, stage in stages
+        for step in range(heads)
+    ):
+        stage(step)
     value = resid[...]
     for step in range(1, heads):
         zo_copies[step - 1].wait_recv()
@@ -440,7 +463,8 @@
         and sides * groups <= LANES
         and rows_here % 16 == 0
         and q_new.shape[1] == heads * rows_here
-        and q_new.shape[2] % CHUNK == 0
+        and args[3].shape[2] % LANES == 0
+        and args[7].shape[1] % CHUNK == 0
         and hidden_in.shape[2] % (2 * CHUNK) == 0
     )
 
@@ -450,10 +474,8 @@
     expert_ids, gate_wts, w_gate, w_up, w_down,
 ):
     sides, groups, heads = (lax.axis_size(name) for name in ("side", "grp", "head"))
-    new_rows = q_new.shape[1]
     rows_here, width = hidden_in.shape[1:]
     half = out_proj.shape[1]
-    chunks = q_new.shape[2] // CHUNK
     operands = (
         q_new, k_cache, value_cache, k_new, new_value_rows, cache_len, hidden_in, out_proj,
         norm_gain.reshape(1, width),
@@ -478,7 +500,7 @@
         out_specs=pl.BlockSpec(memory_space=pltpu.VMEM),
         scratch_shapes=landed
         + [
-            pltpu.VMEM((sides, chunks, new_rows, CHUNK), bf16),
+            pltpu.VMEM((sides, heads, rows_here, q_new.shape[2]), bf16),
             pltpu.VMEM((sides, heads, rows_here, half), bf16),
             pltpu.VMEM((sides, heads, rows_here, half), bf16),
             pltpu.VMEM((rows_here, width), jnp.float32),
@@ -492,7 +514,7 @@
             pltpu.VMEM((heads, rows_here, width), bf16),
             pltpu.VMEM((heads, rows_here, width), bf16),
             dma((len(landed),)),
-            dma((chunks,)), dma((chunks,)),
+            dma((heads,)), dma((heads,)),
             dma((sides * heads,)), dma((sides * heads,)),
             dma((heads,)), dma((heads,)),
             dma((heads, groups)), dma((heads, groups)),

time: 62.4 us -> 54.9 us (0.88)
  Pallas kernels: 60.1 us -> 52.6 us
    pallas_call x1, Pallas kernels: 60.1 us -> 52.6 us  [shards_dense(): pl.pallas_call(dense_kernel, out_shape=jax.ShapeDtypeStruct(hidden_in.sha...]
where the time goes in v3:
time: 54.9 us; the launch traced here: 54.7 us
  Pallas kernels  52.6 us (96%)
  local copies, waits for them, and re-layouts  1.47 us (3%)
  between operations  0.66 us (1%)
    pallas_call x1, Pallas kernels, shards_dense(): pl.pallas_call(dense_kernel, out_shape=jax.ShapeDtypeStruct(hidden_in.sha...  52.6 us
    unnamed x1, local copies, waits for them, and re-layouts  1.47 us

profile of v3, /device:TPU:0, one launch (start us, length us, event | category | flops | bytes accessed | tf_op | source)
XLA Modules:
  0.0 54.7 jit_solution(16001440648173437831)
XLA Ops:
  0.7 52.6 %shard_map.136 = bf16[1,16,2048]{2,1,0:T(8,128)(2,1)} custom-call(bf16[1,64,1024]{2,1,0:T(8,128)(2,1)} %q_hbm.1, bf16[1,1,512,128]{3,2,1,0:T(8,128)(2,1)} %kc_hbm.1, bf16[1,1,512,128]{3,2,1,0:T(8,128)(2,1)} %vc_hbm.1, bf16[1,64,128]{2,1,0:T(8,128)(2,1)} %kn_hbm.1, bf16[1,64,128]{2,1,0:T(8,128)(2,1)} %vn_hbm.1, s32[1]{0:T(128)S(6)} %copy.16.len_ref, ...), custom_call_target="tpu_custom_call" | custom-call | tf_op jit(solution)/shard_map/pallas_call | solution.py:496
  53.2 1.5 %copy.17 = bf16[1,16,2048]{2,1,0:T(8,128)(2,1)} copy(bf16[1,16,2048]{2,1,0:T(8,128)(2,1)} %shard_map.136) | data formatting | bytes 131072

commit v4 on v3

--- a/solution.py
+++ b/solution.py
@@ -158,6 +158,8 @@
     def behind(step):
         return lax.rem(head + heads - step, heads)
 
+    order = sorted(range(heads), key=lambda step: (min(step, heads - step), step))
+
     loads = [
         pltpu.make_async_copy(src, dst, load_sem.at[i])
         for i, (src, dst) in enumerate(
@@ -237,7 +239,7 @@
             ctx[side, step, :, j * head_dim : (j + 1) * head_dim] = found[
                 j * rows_here : (j + 1) * rows_here
             ]
-        if step == heads - 1:
+        if step == order[-1]:
             pl.semaphore_wait(barrier, len(peers))
         ctx_copies[step] = send(
             ctx.at[side, step], ctx.at[side, step], ctx_send.at[step], ctx_recv.at[step],
@@ -245,7 +247,7 @@
         )
 
     def project_rows(step):
-        if step == heads - 1:
+        if step == order[-1]:
             loads[5].wait()
         ctx_copies[step].wait_recv()
         both = ctx[:, step].reshape(sides * rows_here, ctx.shape[3])
@@ -266,11 +268,11 @@
                 )
             )
 
-    attend_rows(heads - 1)
-    for step in range(heads - 2, -1, -1):
+    attend_rows(order[-1])
+    for ahead_of, step in zip(order[::-1], order[-2::-1]):
         attend_rows(step)
-        project_rows(step + 1)
-    project_rows(0)
+        project_rows(ahead_of)
+    project_rows(order[0])
 
     for load in loads[6:10]:
         load.wait()
@@ -311,7 +313,7 @@
     many = sides * groups * rows_here
 
     def axes(step):
-        return (1, 2) if step % 2 == 0 else (2, 1)
+        return (1, 2) if order.index(step) % 2 == 0 else (2, 1)
 
     def to_group(step, k, origin):
         piece = rows.at[behind(step), side, group(origin)]
@@ -330,7 +332,7 @@
         )
 
     def relayed(step):
-        return step < heads - 1
+        return step != order[-1]
 
     def spread(step):
         if step > 0:
@@ -429,7 +431,7 @@
             )
 
     block = rows.at[head, side, grp]
-    for step in range(1, heads):
+    for step in order[1:]:
         z_copies[step] = send(
             block, block, z_send.at[step], z_recv.at[step], (side, grp, ahead(step))
         )
@@ -438,14 +440,14 @@
         (11, reduce_first), (13, reduce_second),
     )
     for _, _, stage, step in sorted(
-        (delay + 2 * step, delay, stage, step)
+        (delay + 2 * turn, delay, stage, step)
         for delay, stage in stages
-        for step in range(heads)
+        for turn, step in enumerate(order)
     ):
         stage(step)
     value = resid[...]
-    for step in range(1, heads):
-        zo_copies[step - 1].wait_recv()
+    for step, copy in zip(order[1:], zo_copies):
+        copy.wait_recv()
         value += z_in[step].astype(jnp.float32)
     out_ref[0] = value.astype(jnp.bfloat16)
     for copy in started:
@@ -495,7 +497,7 @@
     dma = pltpu.SemaphoreType.DMA
     return pl.pallas_call(
         dense_kernel,
-        out_shape=jax.ShapeDtypeStruct(hidden_in.shape, bf16),
+        out_shape=pltpu.VMEM(hidden_in.shape, bf16),
         in_specs=specs,
         out_specs=pl.BlockSpec(memory_space=pltpu.VMEM),
         scratch_shapes=landed

time: 54.9 us -> 51.1 us (0.931)
  Pallas kernels: 52.6 us -> 49.6 us
  local copies, waits for them, and re-layouts: 1.47 us -> 0.63 us
    pallas_call x1, Pallas kernels: 52.6 us -> 49.6 us  [shards_dense(): pl.pallas_call(dense_kernel, out_shape=pltpu.VMEM(hidden_in.shape, bf16),...]
    unnamed x1, local copies, waits for them, and re-layouts: 1.47 us -> 0.63 us
where the time goes in v4:
time: 51.1 us; the launch traced here: 50.9 us
  Pallas kernels  49.6 us (97%)
  between operations  0.66 us (1%)
  local copies, waits for them, and re-layouts  0.63 us (1%)
    pallas_call x1, Pallas kernels, shards_dense(): pl.pallas_call(dense_kernel, out_shape=pltpu.VMEM(hidden_in.shape, bf16),...  49.6 us

profile of v4, /device:TPU:0, one launch (start us, length us, event | category | flops | bytes accessed | tf_op | source)
XLA Modules:
  0.0 50.9 jit_solution(4848422248804636613)
XLA Ops:
  0.7 49.6 %shard_map.136 = bf16[1,16,2048]{2,1,0:T(8,128)(2,1)S(1)} custom-call(bf16[1,64,1024]{2,1,0:T(8,128)(2,1)} %q_hbm.1, bf16[1,1,512,128]{3,2,1,0:T(8,128)(2,1)} %kc_hbm.1, bf16[1,1,512,128]{3,2,1,0:T(8,128)(2,1)} %vc_hbm.1, bf16[1,64,128]{2,1,0:T(8,128)(2,1)} %kn_hbm.1, bf16[1,64,128]{2,1,0:T(8,128)(2,1)} %vn_hbm.1, s32[1]{0:T(128)S(6)} %copy.17.len_ref, ...), custom_call_target="tpu_custom_call" | custom-call | tf_op jit(solution)/shard_map/pallas_call | solution.py:498
  50.3 0.6 %copy.16 = bf16[1,16,2048]{2,1,0:T(8,128)(2,1)} copy(bf16[1,16,2048]{2,1,0:T(8,128)(2,1)S(1)} %shard_map.136) | data formatting | bytes 131072

commit v5 on v3

--- a/solution.py
+++ b/solution.py
@@ -152,11 +152,19 @@
     def group(k):
         return lax.rem(grp // 2 + k // 2, 2) * 2 + lax.rem(lax.rem(grp, 2) + k % 2, 2)
 
-    def ahead(step):
-        return lax.rem(head + step, heads)
-
-    def behind(step):
-        return lax.rem(head + heads - step, heads)
+    def peer(turn):
+        total = 0
+        for at in range(heads):
+            by_distance = sorted(range(heads), key=lambda other_head: abs(other_head - at))
+            others = [m for m in range(heads) if m != at]
+            weight = math.factorial(heads - 1) // math.prod(at - m for m in others)
+            term = weight * by_distance[turn]
+            for m in others:
+                term = term * (head - m)
+            total = total + term
+        return total // math.factorial(heads - 1)
+
+    by_turn = [head] + [peer(turn) for turn in range(1, heads)]
 
     loads = [
         pltpu.make_async_copy(src, dst, load_sem.at[i])
@@ -175,7 +183,7 @@
     barrier = pltpu.get_barrier_semaphore()
     peers = [(other, grp, head)]
     for step in range(1, heads):
-        peers += [(side, grp, ahead(step)), (other, grp, ahead(step))]
+        peers += [(side, grp, by_turn[step]), (other, grp, by_turn[step])]
     peers += [(side, group(k), head) for k in range(1, groups)]
     for peer in peers:
         pl.semaphore_signal(barrier, inc=1, device_id=peer, device_id_type=MESH)
@@ -190,6 +198,12 @@
         copy.start()
         started.append(copy)
         return copy
+
+    def arrived(ref, recv_sem):
+        pltpu.make_async_remote_copy(
+            src_ref=ref, dst_ref=ref, send_sem=recv_sem, recv_sem=recv_sem,
+            device_id=(other, grp, head), device_id_type=MESH,
+        ).wait_recv()
 
     head_dim = kn.shape[1]
     new_rows, cached = kn.shape[0], kc.shape[0]
@@ -205,10 +219,10 @@
     seen_cached = lax.broadcasted_iota(jnp.int32, (many_queries, cached), 1) < valid
     row_pos = lax.rem(lax.broadcasted_iota(jnp.int32, (many_queries, new_rows), 0), rows_here)
     new_pos = lax.broadcasted_iota(jnp.int32, (many_queries, new_rows), 1) - row_pos
-    ctx_copies, part_copies = [None] * heads, []
+    ctx_copies = [None] * heads
 
     def attend_rows(step):
-        start = pl.multiple_of(ahead(step) * rows_here, rows_here)
+        start = pl.multiple_of(by_turn[step] * rows_here, rows_here)
         queries = jnp.concatenate(
             [
                 q[pl.ds(start, rows_here), j * head_dim : (j + 1) * head_dim]
@@ -259,11 +273,9 @@
                 part_in[side, head] = part[side, 0]
                 continue
             slot = turn * heads + step
-            part_copies.append(
-                send(
-                    part.at[to_side, step], part_in.at[side, head],
-                    part_send.at[slot], part_recv.at[slot], (to_side, grp, ahead(step)),
-                )
+            send(
+                part.at[to_side, step], part_in.at[side, head], part_send.at[slot],
+                part_recv.at[turn * heads + head], (to_side, grp, by_turn[step]),
             )
 
     attend_rows(heads - 1)
@@ -290,8 +302,10 @@
     )
     rows[head, side, grp, :, width:] = table.astype(jnp.bfloat16)
 
-    for copy in part_copies:
-        copy.wait_recv()
+    for step in range(heads):
+        arrived(part_in.at[other, by_turn[step]], part_recv.at[heads + by_turn[step]])
+        if step > 0:
+            arrived(part_in.at[side, by_turn[step]], part_recv.at[by_turn[step]])
     square = jnp.zeros((rows_here, 1), jnp.float32)
     for piece in range(sides):
         columns = slice(piece * half, (piece + 1) * half)
@@ -303,10 +317,9 @@
     inv_norm = lax.rsqrt(square * (1.0 / width) + 1e-06)
     rows[head, side, grp, :, :width] = (resid[...] * inv_norm * gain[...]).astype(jnp.bfloat16)
 
-    z_copies, sib_copies = [None] * heads, [[] for _ in range(heads)]
+    sib_copies = [[] for _ in range(heads)]
     xy_copies = [[None] * groups for _ in range(heads)]
     ys_copies, ya_copies, yb_copies = [None] * heads, [None] * heads, [None] * heads
-    zo_copies = []
     own_expert = side * groups + grp
     many = sides * groups * rows_here
 
@@ -314,14 +327,14 @@
         return (1, 2) if step % 2 == 0 else (2, 1)
 
     def to_group(step, k, origin):
-        piece = rows.at[behind(step), side, group(origin)]
+        piece = rows.at[by_turn[step], side, group(origin)]
         slot = k if origin == 0 else origin ^ k
         xy_copies[step][slot] = send(
             piece, piece, xy_send.at[step, slot], xy_recv.at[step, slot], (side, group(k), head)
         )
 
     def to_core(step, origin):
-        piece = rows.at[behind(step), side, group(origin)]
+        piece = rows.at[by_turn[step], side, group(origin)]
         sib_copies[step].append(
             send(
                 piece, piece, sib_send.at[step, origin], sib_recv.at[step, origin],
@@ -330,11 +343,11 @@
         )
 
     def relayed(step):
-        return step < heads - 1
+        return step < heads // 2
 
     def spread(step):
         if step > 0:
-            z_copies[step].wait_recv()
+            arrived(rows.at[by_turn[step], side, grp], z_recv.at[by_turn[step]])
         first, second = axes(step)
         if not relayed(step):
             to_group(step, 3, 0)
@@ -356,7 +369,7 @@
         to_core(step, 3)
 
     def experts(step):
-        at = behind(step)
+        at = by_turn[step]
         if step == 0:
             for load in loads[10:]:
                 load.wait()
@@ -382,7 +395,7 @@
 
     def reduce_cores(step):
         ys_copies[step].wait_recv()
-        value = y[behind(step), side].astype(jnp.float32) + y_sib[step].astype(jnp.float32)
+        value = y[by_turn[step], side].astype(jnp.float32) + y_sib[step].astype(jnp.float32)
         y_sum[step] = value.astype(jnp.bfloat16)
         first, second = axes(step)
         ya_copies[step] = [
@@ -421,18 +434,14 @@
             resid[...] += value
         else:
             z[step] = value.astype(jnp.bfloat16)
-            zo_copies.append(
-                send(
-                    z.at[step], z_in.at[step], zo_send.at[step], zo_recv.at[step],
-                    (side, grp, behind(step)),
-                )
+            send(
+                z.at[step], z_in.at[head], zo_send.at[step], zo_recv.at[head],
+                (side, grp, by_turn[step]),
             )
 
     block = rows.at[head, side, grp]
     for step in range(1, heads):
-        z_copies[step] = send(
-            block, block, z_send.at[step], z_recv.at[step], (side, grp, ahead(step))
-        )
+        send(block, block, z_send.at[step], z_recv.at[head], (side, grp, by_turn[step]))
     stages = (
         (0, spread), (2, relay), (4, finish), (6, experts), (9, reduce_cores),
         (11, reduce_first), (13, reduce_second),
@@ -445,8 +454,8 @@
         stage(step)
     value = resid[...]
     for step in range(1, heads):
-        zo_copies[step - 1].wait_recv()
-        value += z_in[step].astype(jnp.float32)
+        arrived(z_in.at[by_turn[step]], zo_recv.at[by_turn[step]])
+        value += z_in[by_turn[step]].astype(jnp.float32)
     out_ref[0] = value.astype(jnp.bfloat16)
     for copy in started:
         copy.wait_send()
@@ -495,7 +504,7 @@
     dma = pltpu.SemaphoreType.DMA
     return pl.pallas_call(
         dense_kernel,
-        out_shape=jax.ShapeDtypeStruct(hidden_in.shape, bf16),
+        out_shape=pltpu.VMEM(hidden_in.shape, bf16),
         in_specs=specs,
         out_specs=pl.BlockSpec(memory_space=pltpu.VMEM),
         scratch_shapes=landed

time: 54.9 us -> 54.3 us (0.989)
  local copies, waits for them, and re-layouts: 1.47 us -> 0.63 us
    unnamed x1, local copies, waits for them, and re-layouts: 1.47 us -> 0.63 us
where the time goes in v5:
time: 54.3 us; the launch traced here: 54.1 us
  Pallas kernels  52.8 us (97%)
  between operations  0.66 us (1%)
  local copies, waits for them, and re-layouts  0.63 us (1%)
    pallas_call x1, Pallas kernels, shards_dense(): pl.pallas_call(dense_kernel, out_shape=pltpu.VMEM(hidden_in.shape, bf16),...  52.8 us

profile of v5, /device:TPU:0, one launch (start us, length us, event | category | flops | bytes accessed | tf_op | source)
XLA Modules:
  0.0 54.1 jit_solution(4185588187984677614)
XLA Ops:
  0.7 52.8 %shard_map.136 = bf16[1,16,2048]{2,1,0:T(8,128)(2,1)S(1)} custom-call(bf16[1,64,1024]{2,1,0:T(8,128)(2,1)} %q_hbm.1, bf16[1,1,512,128]{3,2,1,0:T(8,128)(2,1)} %kc_hbm.1, bf16[1,1,512,128]{3,2,1,0:T(8,128)(2,1)} %vc_hbm.1, bf16[1,64,128]{2,1,0:T(8,128)(2,1)} %kn_hbm.1, bf16[1,64,128]{2,1,0:T(8,128)(2,1)} %vn_hbm.1, s32[1]{0:T(128)S(6)} %copy.17.len_ref, ...), custom_call_target="tpu_custom_call" | custom-call | tf_op jit(solution)/shard_map/pallas_call | solution.py:505
  53.5 0.6 %copy.16 = bf16[1,16,2048]{2,1,0:T(8,128)(2,1)} copy(bf16[1,16,2048]{2,1,0:T(8,128)(2,1)S(1)} %shard_map.136) | data formatting | bytes 131072

commit v6 on v4

--- a/solution.py
+++ b/solution.py
@@ -178,7 +178,7 @@
     peers = [(other, grp, head)]
     for step in range(1, heads):
         peers += [(side, grp, ahead(step)), (other, grp, ahead(step))]
-    peers += [(side, group(k), head) for k in range(1, groups)]
+    peers += [(side, group(1), head), (side, group(2), head)]
     for peer in peers:
         pl.semaphore_signal(barrier, inc=1, device_id=peer, device_id_type=MESH)
 
@@ -331,15 +331,10 @@
             )
         )
 
-    def relayed(step):
-        return step != order[-1]
-
     def spread(step):
         if step > 0:
             z_copies[step].wait_recv()
         first, second = axes(step)
-        if not relayed(step):
-            to_group(step, 3, 0)
         to_group(step, first, 0)
         to_group(step, second, 0)
         to_core(step, 0)
@@ -347,8 +342,7 @@
     def relay(step):
         first, second = axes(step)
         xy_copies[step][first].wait_recv()
-        if relayed(step):
-            to_group(step, second, first)
+        to_group(step, second, first)
         to_core(step, first)
         xy_copies[step][second].wait_recv()
         to_core(step, second)
@@ -386,24 +380,17 @@
         ys_copies[step].wait_recv()
         value = y[behind(step), side].astype(jnp.float32) + y_sib[step].astype(jnp.float32)
         y_sum[step] = value.astype(jnp.bfloat16)
-        first, second = axes(step)
+        first, _ = axes(step)
         ya_copies[step] = [
             send(
                 y_sum.at[step, group(k)], y_a.at[step, i], ya_send.at[step, i],
-                ya_recv.at[step, i], (side, group(first if relayed(step) else k), head),
+                ya_recv.at[step, i], (side, group(first), head),
             )
             for i, k in enumerate((3, first))
         ]
-        if not relayed(step):
-            yb_copies[step] = send(
-                y_sum.at[step, group(second)], y_b.at[step], yb_send.at[step],
-                yb_recv.at[step], (side, group(second), head),
-            )
 
     def reduce_first(step):
         ya_copies[step][0].wait_recv()
-        if not relayed(step):
-            return
         _, second = axes(step)
         value = y_sum[step, group(second)].astype(jnp.float32) + y_a[step, 0].astype(jnp.float32)
         y_fwd[step] = value.astype(jnp.bfloat16)
@@ -417,8 +404,6 @@
         yb_copies[step].wait_recv()
         value = y_sum[step, grp].astype(jnp.float32) + y_a[step, 1].astype(jnp.float32)
         value += y_b[step].astype(jnp.float32)
-        if not relayed(step):
-            value += y_a[step, 0].astype(jnp.float32)
         if step == 0:
             resid[...] += value
         else:

time: 51.1 us -> 49.3 us (0.965)
  Pallas kernels: 49.6 us -> 47.9 us
    pallas_call x1, Pallas kernels: 49.6 us -> 47.9 us  [shards_dense(): pl.pallas_call(dense_kernel, out_shape=pltpu.VMEM(hidden_in.shape, bf16),...]
where the time goes in v6:
time: 49.3 us; the launch traced here: 49.2 us
  Pallas kernels  47.9 us (97%)
  between operations  0.66 us (1%)
  local copies, waits for them, and re-layouts  0.63 us (1%)
    pallas_call x1, Pallas kernels, shards_dense(): pl.pallas_call(dense_kernel, out_shape=pltpu.VMEM(hidden_in.shape, bf16),...  47.9 us

profile of v6, /device:TPU:0, one launch (start us, length us, event | category | flops | bytes accessed | tf_op | source)
XLA Modules:
  0.0 49.2 jit_solution(7833250511285669412)
XLA Ops:
  0.7 47.9 %shard_map.136 = bf16[1,16,2048]{2,1,0:T(8,128)(2,1)S(1)} custom-call(bf16[1,64,1024]{2,1,0:T(8,128)(2,1)} %q_hbm.1, bf16[1,1,512,128]{3,2,1,0:T(8,128)(2,1)} %kc_hbm.1, bf16[1,1,512,128]{3,2,1,0:T(8,128)(2,1)} %vc_hbm.1, bf16[1,64,128]{2,1,0:T(8,128)(2,1)} %kn_hbm.1, bf16[1,64,128]{2,1,0:T(8,128)(2,1)} %vn_hbm.1, s32[1]{0:T(128)S(6)} %copy.17.len_ref, ...), custom_call_target="tpu_custom_call" | custom-call | tf_op jit(solution)/shard_map/pallas_call | solution.py:483
  48.5 0.6 %copy.16 = bf16[1,16,2048]{2,1,0:T(8,128)(2,1)} copy(bf16[1,16,2048]{2,1,0:T(8,128)(2,1)S(1)} %shard_map.136) | data formatting | bytes 131072
